TPU v7x, 128 devices: a whole 4x4x4 slice. The times are simulated.
128 devices in a mesh: rows: 32 (over x, y, core), cols: 4 (over z).
Axes of the slice: x: 4, y: 4, z: 4, core: 2. Of those that a mesh axis runs over, the one named last changes fastest.
Arguments:
- trace_values: float32 [32, 2097152], P('cols', 'rows'), may hold values from -6 to 6
- challenges: float32 [32], P('cols'), may hold values from 0.5 to 4
- multiplicity: int32 [32, 4194304], P('cols', 'rows'), may hold values from 0 to 3
- table_index: int32 [32, 4194304], P('cols', 'rows'), may hold values from 0 to 8187
Outputs:
- extended: float32 [32, 4194304], P('cols', 'rows')
- fraction: float32 [4194304], P(('rows', 'cols'))
- running: float32 [4194304], P(('rows', 'cols'))
All inputs are finite; a program needn't handle non-finite values.
Results may differ from a plain program's by a relative error of at most 0.000068.
Values sent between devices are 32-bit elements; how exact they have to be, the bound alone decides.
A program may use at most 192 MiB of HBM per device.

v0:
```python
import functools
import math

import jax
import jax.numpy as jnp
import ml_dtypes
import numpy as np
from jax import lax
from jax.experimental import pallas as pl
from jax.experimental.pallas import tpu as pltpu
from jax.sharding import PartitionSpec as P

TABLE_ROWS = 8188
NODES = 16
LEAF = 128
RADIX = 16
LANES = 128
MESH = pl.DeviceIdType.MESH
HIGHEST = lax.Precision.HIGHEST
F32 = jnp.float32
BF16 = jnp.bfloat16


def chebyshev():
    return np.cos((2 * np.arange(NODES) + 1) * np.pi / (2 * NODES))


def lagrange(places):
    order = np.arange(1, NODES)
    waves = np.cos(order * np.arccos(np.clip(places, -1, 1))[..., None])
    at_nodes = np.cos(order * np.arccos(chebyshev())[:, None])
    return (1 + 2 * waves @ at_nodes.T) / NODES


def sign(index):
    return 1.0 - 2.0 * (index % 2)


def cotangent(offset, total):
    return 1.0 / np.tan(np.pi * offset / total) / total


def point_to_moment():
    rows = np.arange(LEAF)
    return sign(rows)[:, None] * lagrange((rows - LEAF / 2) / (LEAF / 2))


def local_to_point():
    rows = np.arange(LEAF)
    return (sign(rows)[:, None] * lagrange((rows + 0.5 - LEAF / 2) / (LEAF / 2))).T


def child_to_parent():
    child = np.arange(RADIX)[:, None]
    return lagrange((2 * child + 1 + chebyshev()[None]) / RADIX - 1).reshape(RADIX * NODES, NODES)


def far_weights(sources, targets, width, total, blocks):
    nodes = chebyshev()
    apart = (targets[None, :] - sources[:, None])[:, None, :, None]
    offset = width * apart + width / 2 * (nodes[None, None, None, :] - nodes[None, :, None, None])
    far = np.abs(apart) >= 2
    if blocks:
        far = far & (np.abs(apart) <= blocks - 2)
    far = np.broadcast_to(far, offset.shape)
    weights = np.where(far, cotangent(np.where(far, offset, 1.0), total), 0.0)
    return weights.reshape(sources.size * NODES, targets.size * NODES)


def near_weights(total):
    source = np.arange(3 * LEAF)[:, None] - LEAF
    target = np.arange(LEAF)[None, :]
    return sign(target - source) * cotangent(target - source + 0.5, total)


def split(matrix):
    high = matrix.astype(np.float32).astype(ml_dtypes.bfloat16)
    low = (matrix - high.astype(np.float64)).astype(np.float32).astype(ml_dtypes.bfloat16)
    return high, low


def matrices(total, groups):
    middle = LEAF * RADIX
    top = middle * RADIX
    blocks = total // top
    per_device = blocks // groups
    p2m = point_to_moment()
    packed = np.zeros((RADIX, LEAF, RADIX, NODES))
    for leaf in range(RADIX):
        packed[leaf, :, leaf, :] = p2m
    c2p = child_to_parent()
    three = np.arange(3 * RADIX) - RADIX
    one = np.arange(RADIX)
    top_far = np.zeros((blocks * NODES, LANES))
    top_far[:, : per_device * NODES] = far_weights(
        np.arange(blocks), np.arange(per_device), top, total, blocks
    )
    top_down = np.zeros((LANES, per_device * RADIX * NODES))
    for block in range(per_device):
        at = slice(block * NODES, (block + 1) * NODES)
        top_down[at, block * RADIX * NODES : (block + 1) * RADIX * NODES] = c2p.T
    out = np.zeros((4 * LEAF, 2 * LEAF))
    out[: 3 * LEAF, 1::2] = near_weights(total)
    out[LEAF + np.arange(LEAF), 2 * np.arange(LEAF)] = 1.0
    out[3 * LEAF :, 1::2] = np.tile(local_to_point(), (LEAF // NODES, 1))
    keep = np.zeros((LEAF, 2 * LEAF))
    keep[np.arange(LEAF), 2 * np.arange(LEAF)] = 1.0
    f32 = lambda m: m.astype(np.float32)
    return dict(
        p2m=f32(packed.reshape(RADIX * LEAF, RADIX * NODES)),
        up=f32(np.tile(c2p, (1, RADIX))),
        far0=f32(far_weights(three, one, LEAF, total, 0)),
        far1=f32(far_weights(three, one, middle, total, 0)),
        top=f32(top_far),
        top_down=f32(top_down),
        down=f32(np.tile(c2p.T, (LANES // NODES, 1))),
        out=split(out),
        keep=split(keep)[0],
    )


def dot(left, right):
    return jnp.dot(left, right, preferred_element_type=F32, precision=HIGHEST)


def dot16(left, right):
    return jnp.dot(left, right, preferred_element_type=F32)


def lane_group(rows):
    return lax.broadcasted_iota(jnp.int32, (rows, LANES), 1) // NODES


def spread(local):
    group = lane_group(8)
    half = LANES // NODES
    tiles = []
    for child in range(RADIX):
        tile = local[:, (child // half) * LANES : (child // half + 1) * LANES]
        tiles.append(jnp.where(group == child % half, tile, 0.0))
    return jnp.concatenate(tiles, axis=0)


def gather_children(copies):
    group = lax.broadcasted_iota(jnp.int32, (8, RADIX * NODES), 1) // NODES
    total = jnp.zeros((8, RADIX * NODES), F32)
    for child in range(RADIX):
        total = jnp.where(group == child, copies[8 * child : 8 * child + 8], total)
    return total


def column_sums(tiles):
    row = lax.broadcasted_iota(jnp.int32, (8, LANES), 0)
    for shift in (1, 2, 4):
        first = (row // shift) % 2 == 0
        tiles = [
            jnp.where(first, a, b) + pltpu.roll(jnp.where(first, b, a), shift, 0)
            for a, b in zip(tiles[0::2], tiles[1::2])
        ]
    return tiles[0]


def invert(value):
    guess = pl.reciprocal(value, approx=True)
    return guess * (2.0 - value * guess)


def challenge_tile(challenge_ref):
    row = lax.broadcasted_iota(jnp.int32, (8, LANES), 0)
    tile = jnp.zeros((8, LANES), F32)
    for column in range(8):
        tile = jnp.where(row == column, challenge_ref[column], tile)
    return tile


def greet(axes):
    barrier = pltpu.get_barrier_semaphore()
    for axis, size in axes:
        me = lax.axis_index(axis)

        @pl.loop(1, size)
        def _(step):
            peer = lax.rem(me + step, size)
            pl.semaphore_signal(barrier, inc=1, device_id={axis: peer}, device_id_type=MESH)

    return barrier


def far_kernel(
    groups, challenge_ref, x_hbm, multiplicity_hbm, index_hbm, p2m_ref, up_ref, far0_ref, far1_ref, top_ref,
    top_down_ref, down_ref, local_ref, halo_ref, table_ref,
    x_ref, multiplicity_ref, index_ref, moments_ref, send_ref, gathered_ref, edge_send, edge_recv,
    load_sem, send_sem, recv_sem, edge_send_sem, edge_recv_sem,
):
    me = lax.axis_index("rows")
    rows = x_ref.shape[1]
    parents = rows // (LEAF * RADIX)
    tops = parents // RADIX
    loads = [
        pltpu.make_async_copy(source, target, load_sem.at[k])
        for k, (source, target) in enumerate(
            ((x_hbm, x_ref), (multiplicity_hbm, multiplicity_ref), (index_hbm, index_ref))
        )
    ]
    for load in loads:
        load.start()
    barrier = greet((("rows", groups),))
    loads[0].wait()

    span = LEAF * RADIX
    total = jnp.zeros((8 * parents, RADIX * NODES), F32)
    for part in range(span // 256):
        left = jnp.concatenate(
            [x_ref[:, span * p + 256 * part : span * p + 256 * part + 256] for p in range(parents)], axis=0
        )
        total = total + dot(left, p2m_ref[256 * part : 256 * part + 256, :])
    moments_ref[...] = total
    copies = dot(total, up_ref[...])
    middle = [gather_children(copies[128 * g : 128 * g + 128]) for g in range(tops)]
    high = dot(jnp.concatenate(middle, axis=0), up_ref[:, :LANES])
    group = lane_group(8)
    packed = high[0:8]
    for g in range(1, tops):
        packed = jnp.where(group % tops == g, high[8 * g : 8 * g + 8], packed)
    send_ref[...] = packed
    wide = RADIX * NODES
    edge_send[0, :, 0:LEAF] = x_ref[:, rows - LEAF : rows]
    edge_send[0, :, LEAF : LEAF + wide] = total[8 * (parents - 1) : 8 * parents]
    edge_send[0, :, LEAF + wide :] = middle[tops - 1]
    edge_send[1, :, 0:LEAF] = x_ref[:, 0:LEAF]
    edge_send[1, :, LEAF : LEAF + wide] = total[0:8]
    edge_send[1, :, LEAF + wide :] = middle[0]

    pl.semaphore_wait(barrier, groups - 1)

    def edge(k):
        peer = lax.rem(me + (1 if k == 0 else groups - 1), groups)
        return pltpu.make_async_remote_copy(
            src_ref=edge_send.at[k], dst_ref=edge_recv.at[k], send_sem=edge_send_sem.at[k],
            recv_sem=edge_recv_sem.at[k], device_id={"rows": peer}, device_id_type=MESH,
        )

    def message(step):
        peer = lax.rem(me + groups - step, groups)
        return pltpu.make_async_remote_copy(
            src_ref=send_ref, dst_ref=gathered_ref.at[step], send_sem=send_sem.at[step],
            recv_sem=recv_sem.at[step], device_id={"rows": peer}, device_id_type=MESH,
        )

    @pl.loop(1, groups)
    def _(step):
        message(step).start()

    edge(0).start()
    edge(1).start()

    loads[1].wait()
    loads[2].wait()
    weight = challenge_tile(challenge_ref)

    @pl.loop(0, index_ref.shape[1] // 1024)
    def _(k):
        tiles = []
        for tile in range(8):
            at = pl.ds(pl.multiple_of(k * 1024 + tile * LANES, LANES), LANES)
            value = (index_ref[:, at].astype(F32) - TABLE_ROWS / 2) * (8.0 / TABLE_ROWS)
            tiles.append(multiplicity_ref[:, at].astype(F32) * invert(weight + value * value))
        table_ref[pl.ds(pl.multiple_of(8 * k, 8), 8), :] = column_sums(tiles)

    gathered_ref[0] = send_ref[...]

    @pl.loop(1, groups)
    def _(step):
        message(step).wait()

    edge(0).wait()
    edge(1).wait()
    per_tile = LANES // (tops * NODES)
    pieces = []
    for k in range(groups // per_tile):
        tile = gathered_ref[per_tile * k]
        for place in range(1, per_tile):
            tile = jnp.where(group // tops == place, gathered_ref[per_tile * k + place], tile)
        pieces.append(tile)
    top_local = dot(jnp.concatenate(pieces, axis=1), top_ref[...])
    from_top = dot(top_local, top_down_ref[...])
    line = [edge_recv[0, :, LEAF + wide :]] + middle + [edge_recv[1, :, LEAF + wide :]]
    left = jnp.concatenate([jnp.concatenate(line[g : g + 3], axis=1) for g in range(tops)], axis=0)
    middle_local = dot(left, far1_ref[...])
    middle_local = [
        middle_local[8 * g : 8 * g + 8] + from_top[:, wide * g : wide * g + wide] for g in range(tops)
    ]
    moments = moments_ref[...]
    before = jnp.concatenate([edge_recv[0, :, LEAF : LEAF + wide], moments[:-8]], axis=0)
    after = jnp.concatenate([moments[8:], edge_recv[1, :, LEAF : LEAF + wide]], axis=0)
    local = dot(before, far0_ref[0:wide]) + dot(moments, far0_ref[wide : 2 * wide])
    local = local + dot(after, far0_ref[2 * wide :])
    local_ref[...] = local + dot(
        jnp.concatenate([spread(m) for m in middle_local], axis=0), down_ref[...]
    )
    halo_ref[0] = edge_recv[0, :, 0:LEAF]
    halo_ref[1] = edge_recv[1, :, 0:LEAF]


def two(value):
    high = value.astype(BF16)
    return high, (value - high.astype(F32)).astype(BF16)


def rows_kernel(
    challenge_ref, x_ref, halo_ref, local_ref, table_ref, high_ref, low_ref, keep_ref, extended_ref, partial_ref
):
    step = pl.program_id(0)
    steps = pl.num_programs(0)
    rows = x_ref.shape[1] // steps
    leaves = rows // LEAF
    start = pl.multiple_of(step * rows, rows)
    before = pl.multiple_of(jnp.maximum(start - LEAF, 0), LEAF)
    after = pl.multiple_of(jnp.minimum(start + rows, x_ref.shape[1] - LEAF), LEAF)
    tiles = [jnp.where(step == 0, halo_ref[0], x_ref[:, pl.ds(before, LEAF)])]
    for leaf in range(leaves):
        tiles.append(x_ref[:, pl.ds(pl.multiple_of(start + leaf * LEAF, LEAF), LEAF)])
    tiles.append(jnp.where(step == steps - 1, halo_ref[1], x_ref[:, pl.ds(after, LEAF)]))
    values = jnp.concatenate(tiles, axis=0)
    local = local_ref[...]
    sources = [values[8 * k : 8 * k + 8 * leaves] for k in range(3)]
    sources.append(
        jnp.concatenate([spread(local[8 * p : 8 * p + 8]) for p in range(leaves // RADIX)], axis=0)
    )
    pairs = [two(source) for source in sources]
    high = jnp.concatenate([pair[0] for pair in pairs], axis=1)
    low = jnp.concatenate([pair[1] for pair in pairs], axis=1)
    own = sources[1]
    rest = (own - pairs[1][0].astype(F32) - pairs[1][1].astype(F32)).astype(BF16)
    result = dot16(rest, keep_ref[...]) + dot16(low, high_ref[...])
    result = result + dot16(high, low_ref[...]) + dot16(high, high_ref[...])
    weight = challenge_tile(challenge_ref)
    terms = []
    for leaf in range(leaves):
        both = result[8 * leaf : 8 * leaf + 8]
        extended_ref[:, 2 * LEAF * leaf : 2 * LEAF * leaf + 2 * LEAF] = both
        for half in range(2):
            value = both[:, LANES * half : LANES * half + LANES]
            terms.append(invert(weight + value * value))
    for k in range(len(terms) // 8):
        partial_ref[8 * k : 8 * k + 8, :] = column_sums(terms[8 * k : 8 * k + 8]) - table_ref[8 * k : 8 * k + 8, :]


def sums_kernel(
    groups, parts, scale, partial_ref, lane_ref, row_ref, fraction_ref, running_ref,
    pieces_ref, note_ref, notes_ref, entry_ref, entries_ref,
    piece_send, piece_recv, note_send, note_recv, entry_send, entry_recv,
):
    me = lax.axis_index("rows")
    part = lax.axis_index("cols")
    size = partial_ref.shape[0] // parts
    barrier = greet((("rows", groups), ("cols", parts)))
    totals = []
    for p in range(parts):
        totals.append(jnp.sum(partial_ref[size * p : size * p + size, :]))
    note_ref[...] = jnp.full(note_ref.shape, sum(totals[1:], totals[0]), F32)
    pl.semaphore_wait(barrier, groups + parts - 2)

    def piece(step):
        peer = lax.rem(part + parts - step, parts)
        return pltpu.make_async_remote_copy(
            src_ref=partial_ref.at[pl.ds(pl.multiple_of(peer * size, size), size)], dst_ref=pieces_ref.at[step],
            send_sem=piece_send.at[step], recv_sem=piece_recv.at[step], device_id={"cols": peer},
            device_id_type=MESH,
        )

    def note(step):
        peer = lax.rem(me + groups - step, groups)
        return pltpu.make_async_remote_copy(
            src_ref=note_ref, dst_ref=notes_ref.at[step], send_sem=note_send.at[step],
            recv_sem=note_recv.at[step], device_id={"rows": peer}, device_id_type=MESH,
        )

    def entry(step):
        peer = lax.rem(part + parts - step, parts)
        return pltpu.make_async_remote_copy(
            src_ref=entry_ref.at[peer], dst_ref=entries_ref.at[step], send_sem=entry_send.at[step],
            recv_sem=entry_recv.at[step], device_id={"cols": peer}, device_id_type=MESH,
        )

    @pl.loop(1, groups)
    def _(step):
        note(step).start()

    @pl.loop(1, parts)
    def _(step):
        piece(step).start()

    @pl.loop(1, groups)
    def _(step):
        note(step).wait()

    entering = jnp.zeros(note_ref.shape, F32)
    for step in range(1, groups):
        entering = entering + jnp.where(me + step >= groups, notes_ref[step], 0.0)
    for p in range(parts):
        entry_ref[p] = entering
        entering = entering + totals[p]

    @pl.loop(1, parts)
    def _(step):
        entry(step).start()

    @pl.loop(1, parts)
    def _(step):
        piece(step).wait()

    own = partial_ref[pl.ds(pl.multiple_of(part * size, size), size), :]
    for step in range(1, parts):
        own = own + pieces_ref[step]
    fraction_ref[...] = own
    within = dot(own, lane_ref[...])
    rows_before = dot(row_ref[...], jnp.broadcast_to(within[:, LANES - 1 :], within.shape))

    @pl.loop(1, parts)
    def _(step):
        entry(step).wait()

    carry = entry_ref[part]
    for step in range(1, parts):
        carry = carry + entries_ref[step]
    running_ref[...] = (within + rows_before + carry[0:1]) * scale


def local(groups, parts, trace_values, challenges, multiplicity, table_index):
    columns, rows = trace_values.shape
    total = groups * rows
    m = matrices(total, groups)
    wide = RADIX * NODES
    parents = rows // (LEAF * RADIX)
    vmem = pl.BlockSpec(memory_space=pltpu.VMEM)
    smem = pl.BlockSpec(memory_space=pltpu.SMEM)
    hbm = pl.BlockSpec(memory_space=pl.ANY)
    dma = pltpu.SemaphoreType.DMA
    sum_rows = 2 * rows // LANES
    far, halo, table = pl.pallas_call(
        functools.partial(far_kernel, groups),
        out_shape=(
            jax.ShapeDtypeStruct((columns * parents, wide), F32),
            jax.ShapeDtypeStruct((2, columns, LEAF), F32),
            jax.ShapeDtypeStruct((sum_rows, LANES), F32),
        ),
        in_specs=[smem, hbm, hbm, hbm] + [vmem] * 7,
        out_specs=(vmem, vmem, vmem),
        scratch_shapes=[
            pltpu.VMEM((columns, rows), F32),
            pltpu.VMEM((columns, 2 * rows), jnp.int32),
            pltpu.VMEM((columns, 2 * rows), jnp.int32),
            pltpu.VMEM((columns * parents, wide), F32),
            pltpu.VMEM((columns, LANES), F32),
            pltpu.VMEM((groups, columns, LANES), F32),
            pltpu.VMEM((2, columns, LEAF + 2 * wide), F32),
            pltpu.VMEM((2, columns, LEAF + 2 * wide), F32),
            dma((3,)), dma((groups,)), dma((groups,)), dma((2,)), dma((2,)),
        ],
        compiler_params=pltpu.CompilerParams(
            collective_id=0, has_side_effects=True, vmem_limit_bytes=48 * 2**20
        ),
        name="far",
    )(
        challenges, trace_values, multiplicity, table_index, m["p2m"], m["up"], m["far0"], m["far1"], m["top"],
        m["top_down"], m["down"],
    )
    steps = parents // 2
    whole = lambda shape: pl.BlockSpec(shape, lambda i: (0,) * len(shape))
    extended, partial = pl.pallas_call(
        rows_kernel,
        grid=(steps,),
        out_shape=(
            jax.ShapeDtypeStruct((columns, 2 * rows), F32),
            jax.ShapeDtypeStruct((sum_rows, LANES), F32),
        ),
        in_specs=[
            smem,
            whole((columns, rows)),
            whole((2, columns, LEAF)),
            pl.BlockSpec((columns * parents // steps, wide), lambda i: (i, 0)),
            pl.BlockSpec((sum_rows // steps, LANES), lambda i: (i, 0)),
            whole((4 * LEAF, 2 * LEAF)),
            whole((4 * LEAF, 2 * LEAF)),
            whole((LEAF, 2 * LEAF)),
        ],
        out_specs=(
            pl.BlockSpec((columns, 2 * rows // steps), lambda i: (0, i)),
            pl.BlockSpec((sum_rows // steps, LANES), lambda i: (i, 0)),
        ),
        compiler_params=pltpu.CompilerParams(vmem_limit_bytes=48 * 2**20),
        name="rows",
    )(challenges, trace_values, halo, far, table, m["out"][0], m["out"][1], m["keep"])
    size = sum_rows // parts
    own = jax.ShapeDtypeStruct((size, LANES), F32)
    lane_sum = np.triu(np.ones((LANES, LANES), np.float32))
    row_sum = np.tril(np.ones((size, size), np.float32), -1)
    fraction, running = pl.pallas_call(
        functools.partial(sums_kernel, groups, parts, 1.0 / (2 * total)),
        out_shape=(own, own),
        in_specs=[vmem, vmem, vmem],
        out_specs=(vmem, vmem),
        scratch_shapes=[
            pltpu.VMEM((parts, size, LANES), F32),
            pltpu.VMEM((8, LANES), F32),
            pltpu.VMEM((groups, 8, LANES), F32),
            pltpu.VMEM((parts, 8, LANES), F32),
            pltpu.VMEM((parts, 8, LANES), F32),
            dma((parts,)), dma((parts,)), dma((groups,)), dma((groups,)), dma((parts,)), dma((parts,)),
        ],
        compiler_params=pltpu.CompilerParams(
            collective_id=1, has_side_effects=True, vmem_limit_bytes=32 * 2**20
        ),
        name="sums",
    )(partial, lane_sum, row_sum)
    return extended, fraction.reshape(-1), running.reshape(-1)


def solution(mesh):
    return jax.shard_map(
        functools.partial(local, mesh.shape["rows"], mesh.shape["cols"]),
        mesh=mesh,
        in_specs=(P("cols", "rows"), P("cols"), P("cols", "rows"), P("cols", "rows")),
        out_specs=(P("cols", "rows"), P(("rows", "cols")), P(("rows", "cols"))),
        check_vma=False,
    )
```

profile of v0, /device:TPU:1, one launch (start us, length us, event | category | flops | bytes accessed | tf_op | source)
XLA Modules:
  0.0 54.6 jit_solution(8341467549736134961)
XLA Ops:
  0.6 0.0 copy-start
  0.6 1.6 %copy-done = f32[8,65536]{1,0:T(8,128)S(1)} copy-done((f32[8,65536]{1,0:T(8,128)S(1)}, f32[8,65536]{1,0:T(8,128)}, u32[]{:S(2)}) %copy-start) | copy-done | bytes 2097176
  2.2 0.0 copy-start.1
  2.2 1.1 %copy-done.1 = f32[768,256]{1,0:T(8,128)S(1)} copy-done((f32[768,256]{1,0:T(8,128)S(1)}, f32[768,256]{1,0:T(8,128)}, u32[]{:S(2)}) %copy-start.1) | copy-done | bytes 786456
  3.4 0.0 copy-start.2
  3.4 1.1 %copy-done.2 = f32[768,256]{1,0:T(8,128)S(1)} copy-done((f32[768,256]{1,0:T(8,128)S(1)}, f32[768,256]{1,0:T(8,128)}, u32[]{:S(2)}) %copy-start.2) | copy-done | bytes 786456
  4.5 0.0 copy-start.3
  4.5 1.0 %copy-done.3 = f32[1024,128]{1,0:T(8,128)S(1)} copy-done((f32[1024,128]{1,0:T(8,128)S(1)}, f32[1024,128]{1,0:T(8,128)}, u32[]{:S(2)}) %copy-start.3) | copy-done | bytes 524312
  5.5 0.0 copy-start.4
  5.5 0.9 %copy-done.4 = f32[128,512]{1,0:T(8,128)S(1)} copy-done((f32[128,512]{1,0:T(8,128)S(1)}, f32[128,512]{1,0:T(8,128)}, u32[]{:S(2)}) %copy-start.4) | copy-done | bytes 262168
  6.5 0.0 copy-start.5
  6.5 0.9 %copy-done.5 = f32[256,256]{1,0:T(8,128)S(1)} copy-done((f32[256,256]{1,0:T(8,128)S(1)}, f32[256,256]{1,0:T(8,128)}, u32[]{:S(2)}) %copy-start.5) | copy-done | bytes 262168
  7.4 0.0 copy-start.9
  7.4 0.9 %copy-done.9 = f32[128,256]{1,0:T(8,128)S(1)} copy-done((f32[128,256]{1,0:T(8,128)S(1)}, f32[128,256]{1,0:T(8,128)}, u32[]{:S(2)}) %copy-start.9) | copy-done | bytes 131096
  8.3 0.0 copy-start.12
  8.3 0.7 %copy-done.12 = f32[8]{0:T(128)S(1)} copy-done((f32[8]{0:T(128)S(1)}, f32[8]{0:T(128)}, u32[]{:S(2)}) %copy-start.12) | copy-done | bytes 56
  9.0 0.0 copy-start.6
  9.0 0.0 copy-start.7
  9.0 0.0 copy-start.10
  9.0 0.0 copy-start.8
  9.0 0.0 copy-start.11
  9.0 19.0 %far.1 = (f32[256,256]{1,0:T(8,128)S(1)}, f32[2,8,128]{2,1,0:T(8,128)S(1)}, f32[1024,128]{1,0:T(8,128)S(1)}) custom-call(f32[8]{0:T(128)S(1)} %copy-done.12, f32[8,65536]{1,0:T(8,128)S(1)} %copy-done, s32[8,131072]{1,0:T(8,128)} %multiplicity_hbm.1, s32[8,131072]{1,0:T(8,128)} %index_hbm.1, f32[2048,256]{1,0:T(8,128)} %constant.24.clone.p2m_ref, ...), custom_call_target="tpu_custom_call" | custom-call | tf_op jit(solution)/shard_map/far/pallas_call | solution.py:441
  28.0 0.0 copy-done.6
  28.1 0.0 copy-done.7
  28.1 0.0 copy-done.10
  28.1 10.1 %rows.1 = (f32[8,131072]{1,0:T(8,128)}, f32[1024,128]{1,0:T(8,128)S(1)}) custom-call(f32[8]{0:T(128)S(1)} %copy-done.12, f32[8,65536]{1,0:T(8,128)S(1)} %copy-done, f32[2,8,128]{2,1,0:T(8,128)S(1)} %get-tuple-element.10.halo_ref, f32[256,256]{1,0:T(8,128)S(1)} %get-tuple-element.11.local_ref, f32[1024,128]{1,0:T(8,128)S(1)} %get-tuple-element.12.table_ref, ...), custom_call_target="tpu_custom_call" | custom-call | tf_op jit(solution)/shard_map/rows/pallas_call | solution.py:471
  38.1 0.0 copy-done.8
  38.1 0.0 copy-done.11
  38.1 15.2 %sums.1 = (f32[256,128]{1,0:T(8,128)S(1)}, f32[256,128]{1,0:T(8,128)S(1)}) custom-call(f32[1024,128]{1,0:T(8,128)S(1)} %get-tuple-element.14.partial_ref, f32[128,128]{1,0:T(8,128)S(1)} %copy-done.11, f32[256,256]{1,0:T(8,128)S(1)} %copy-done.8), custom_call_target="tpu_custom_call" | custom-call | tf_op jit(solution)/shard_map/sums/pallas_call | solution.py:499
  53.3 0.7 %copy.21 = f32[32768]{0:T(1024)} copy(f32[32768]{0:T(1024)S(1)} %bitcast.3) | data formatting | bytes 262144
  54.0 0.7 %copy.22 = f32[32768]{0:T(1024)} copy(f32[32768]{0:T(1024)S(1)} %bitcast.2) | data formatting | bytes 262144
Async XLA Ops:
  0.6 1.6 %copy-start = (f32[8,65536]{1,0:T(8,128)S(1)}, f32[8,65536]{1,0:T(8,128)}, u32[]{:S(2)}) copy-start(f32[8,65536]{1,0:T(8,128)} %x_ref.1) | copy-start | bytes 6291460
  2.2 1.1 %copy-start.1 = (f32[768,256]{1,0:T(8,128)S(1)}, f32[768,256]{1,0:T(8,128)}, u32[]{:S(2)}) copy-start(f32[768,256]{1,0:T(8,128)} %constant.27.clone.far1_ref) | copy-start | bytes 2359300
  3.4 1.1 %copy-start.2 = (f32[768,256]{1,0:T(8,128)S(1)}, f32[768,256]{1,0:T(8,128)}, u32[]{:S(2)}) copy-start(f32[768,256]{1,0:T(8,128)} %constant.26.clone.far0_ref) | copy-start | bytes 2359300
  4.5 1.0 %copy-start.3 = (f32[1024,128]{1,0:T(8,128)S(1)}, f32[1024,128]{1,0:T(8,128)}, u32[]{:S(2)}) copy-start(f32[1024,128]{1,0:T(8,128)} %constant.28.clone.top_ref) | copy-start | bytes 1572868
  5.5 0.9 %copy-start.4 = (f32[128,512]{1,0:T(8,128)S(1)}, f32[128,512]{1,0:T(8,128)}, u32[]{:S(2)}) copy-start(f32[128,512]{1,0:T(8,128)} %constant.29.clone.top_down_ref) | copy-start | bytes 786436
  6.5 0.9 %copy-start.5 = (f32[256,256]{1,0:T(8,128)S(1)}, f32[256,256]{1,0:T(8,128)}, u32[]{:S(2)}) copy-start(f32[256,256]{1,0:T(8,128)} %constant.25.clone.up_ref) | copy-start | bytes 786436
  7.4 0.9 %copy-start.9 = (f32[128,256]{1,0:T(8,128)S(1)}, f32[128,256]{1,0:T(8,128)}, u32[]{:S(2)}) copy-start(f32[128,256]{1,0:T(8,128)} %constant.30.clone.down_ref) | copy-start | bytes 393220
  8.3 0.7 %copy-start.12 = (f32[8]{0:T(128)S(1)}, f32[8]{0:T(128)}, u32[]{:S(2)}) copy-start(f32[8]{0:T(128)} %challenge_ref.3) | copy-start | bytes 100
  9.0 19.1 %copy-start.6 = (bf16[512,256]{1,0:T(8,128)(2,1)S(1)}, bf16[512,256]{1,0:T(8,128)(2,1)}, u32[]{:S(2)}) copy-start(bf16[512,256]{1,0:T(8,128)(2,1)} %constant.32.clone.low_ref) | copy-start | bytes 786436
  9.0 19.1 %copy-start.7 = (bf16[512,256]{1,0:T(8,128)(2,1)S(1)}, bf16[512,256]{1,0:T(8,128)(2,1)}, u32[]{:S(2)}) copy-start(bf16[512,256]{1,0:T(8,128)(2,1)} %constant.31.clone.high_ref) | copy-start | bytes 786436
  9.0 19.1 %copy-start.10 = (bf16[128,256]{1,0:T(8,128)(2,1)S(1)}, bf16[128,256]{1,0:T(8,128)(2,1)}, u32[]{:S(2)}) copy-start(bf16[128,256]{1,0:T(8,128)(2,1)} %constant.33.clone.keep_ref) | copy-start | bytes 196612
  9.0 29.1 %copy-start.8 = (f32[256,256]{1,0:T(8,128)S(1)}, f32[256,256]{1,0:T(8,128)}, u32[]{:S(2)}) copy-start(f32[256,256]{1,0:T(8,128)} %constant.35.clone.row_ref) | copy-start | bytes 786436
  9.0 29.1 %copy-start.11 = (f32[128,128]{1,0:T(8,128)S(1)}, f32[128,128]{1,0:T(8,128)}, u32[]{:S(2)}) copy-start(f32[128,128]{1,0:T(8,128)} %constant.34.clone.lane_ref) | copy-start | bytes 196612
where the time goes:
time: 55 us; the launch traced here: 54.6 us
  Pallas kernels  44.3 us (81%)
  local copies, waits for them, and re-layouts  9.7 us (18%)
  between operations  0.7 us (1%)
    pallas_call x1, Pallas kernels, local(): pl.pallas_call(functools.partial(far_kernel, groups), out_shape=(jax.Shap...  19 us
    pallas_call x1, Pallas kernels, local(): pl.pallas_call(functools.partial(sums_kernel, groups, parts, 1.0 / (2 * t...  15.2 us
    pallas_call x1, Pallas kernels, local(): pl.pallas_call(rows_kernel, grid=(steps,), out_shape=(jax.ShapeDtypeStruc...  10.1 us
    unnamed x28, local copies, waits for them, and re-layouts  9.7 us

commit v1 on v0

v1 whole, which is shorter than its diff:
```python
import functools
import math

import jax
import jax.numpy as jnp
import ml_dtypes
import numpy as np
from jax import lax
from jax.experimental import pallas as pl
from jax.experimental.pallas import tpu as pltpu
from jax.sharding import PartitionSpec as P

TABLE_ROWS = 8188
NODES = 16
LEAF = 128
RADIX = 16
LANES = 128
WIDE = RADIX * NODES
BATCH = 4
MESH = pl.DeviceIdType.MESH
F32 = jnp.float32
BF16 = jnp.bfloat16


def chebyshev():
    return np.cos((2 * np.arange(NODES) + 1) * np.pi / (2 * NODES))


def lagrange(places):
    order = np.arange(1, NODES)
    waves = np.cos(order * np.arccos(np.clip(places, -1, 1))[..., None])
    at_nodes = np.cos(order * np.arccos(chebyshev())[:, None])
    return (1 + 2 * waves @ at_nodes.T) / NODES


def sign(index):
    return 1.0 - 2.0 * (index % 2)


def cotangent(offset, total):
    return 1.0 / np.tan(np.pi * offset / total) / total


def point_to_moment():
    rows = np.arange(LEAF)
    return sign(rows)[:, None] * lagrange((rows - LEAF / 2) / (LEAF / 2))


def local_to_point():
    rows = np.arange(LEAF)
    return (sign(rows)[:, None] * lagrange((rows + 0.5 - LEAF / 2) / (LEAF / 2))).T


def child_to_parent():
    child = np.arange(RADIX)[:, None]
    return lagrange((2 * child + 1 + chebyshev()[None]) / RADIX - 1).reshape(RADIX * NODES, NODES)


def far_weights(sources, targets, width, total, blocks):
    nodes = chebyshev()
    apart = (targets[None, :] - sources[:, None])[:, None, :, None]
    offset = width * apart + width / 2 * (nodes[None, None, None, :] - nodes[None, :, None, None])
    far = np.abs(apart) >= 2
    if blocks:
        far = far & (np.abs(apart) <= blocks - 2)
    far = np.broadcast_to(far, offset.shape)
    weights = np.where(far, cotangent(np.where(far, offset, 1.0), total), 0.0)
    return weights.reshape(sources.size * NODES, targets.size * NODES)


def split(matrix):
    high = matrix.astype(np.float32).astype(ml_dtypes.bfloat16)
    low = (matrix - high.astype(np.float64)).astype(np.float32).astype(ml_dtypes.bfloat16)
    return high, low


def matrices(total, groups):
    middle = LEAF * RADIX
    top = middle * RADIX
    blocks = total // top
    per_device = blocks // groups
    c2p = child_to_parent()
    three = np.arange(3 * RADIX) - RADIX
    one = np.arange(RADIX)
    top_far = np.zeros((blocks * NODES, WIDE))
    top_far[:, : per_device * NODES] = far_weights(
        np.arange(blocks), np.arange(per_device), top, total, blocks
    )
    top_down = np.zeros((per_device, LANES, WIDE))
    for block in range(per_device):
        top_down[block, block * NODES : (block + 1) * NODES] = c2p.T
    source = np.arange(4 * LEAF)[:, None] - LEAF
    target = np.arange(2 * LEAF)[None, :]
    near = sign(target - source) * cotangent(target - source + 0.5, total)
    near = np.where(np.abs(target // LEAF - source // LEAF) <= 1, near, 0.0)
    child_out = np.zeros((LANES // NODES, NODES, 2, LEAF))
    for child in range(LANES // NODES):
        child_out[child, :, child % 2] = local_to_point()
    weave = np.zeros((2, LEAF, 2 * LEAF))
    for side in range(2):
        weave[side, np.arange(LEAF), 2 * np.arange(LEAF) + side] = 1.0
    parts = dict(
        p2m=np.tile(point_to_moment(), (1, RADIX)),
        up=np.tile(c2p, (1, RADIX)),
        far0=far_weights(three, one, LEAF, total, 0),
        far1=far_weights(three, one, middle, total, 0),
        top=top_far,
        top_down=top_down.reshape(-1, WIDE),
        down=np.tile(c2p.T, (LANES // NODES, 1)),
        out=np.concatenate([near, child_out.reshape(LANES, WIDE)]),
        weave=weave.reshape(2 * LEAF, WIDE),
    )
    places, start = {}, 0
    for name, part in parts.items():
        places[name] = (start, start + part.shape[0])
        start += part.shape[0]
    return split(np.concatenate(list(parts.values()))), places


def dot16(left, right):
    return jnp.dot(left, right, preferred_element_type=F32)


def two(value):
    high = value.astype(BF16)
    return high, (value - high.astype(F32)).astype(BF16)


def dot_pieces(left, right):
    return dot16(left[1], right[0]) + dot16(left[0], right[1]) + dot16(left[0], right[0])


def dot_exact(left, right):
    high, low = two(left)
    rest = (left - high.astype(F32) - low.astype(F32)).astype(BF16)
    return dot16(rest, right) + dot16(low, right) + dot16(high, right)


def spread(local, span):
    group = lax.broadcasted_iota(jnp.int32, (8, LANES), 1) // span
    half = LANES // span
    tiles = []
    for child in range(WIDE // span):
        tile = local[:, (child // half) * LANES : (child // half + 1) * LANES]
        tiles.append(jnp.where(group == child % half, tile, 0.0))
    return tiles


def gather_children(copies):
    group = lax.broadcasted_iota(jnp.int32, (8, WIDE), 1) // NODES
    total = jnp.zeros((8, WIDE), F32)
    for child in range(RADIX):
        total = jnp.where(group == child, copies[8 * child : 8 * child + 8], total)
    return total


def column_sums(tiles):
    row = lax.broadcasted_iota(jnp.int32, (8, LANES), 0)
    for shift in (1, 2, 4):
        first = (row // shift) % 2 == 0
        tiles = [
            jnp.where(first, a, b) + pltpu.roll(jnp.where(first, b, a), shift, 0)
            for a, b in zip(tiles[0::2], tiles[1::2])
        ]
    return tiles[0]


def invert(value):
    guess = pl.reciprocal(value, approx=True)
    return guess * (2.0 - value * guess)


def challenge_tile(challenge_ref):
    row = lax.broadcasted_iota(jnp.int32, (8, LANES), 0)
    tile = jnp.zeros((8, LANES), F32)
    for column in range(8):
        tile = jnp.where(row == column, challenge_ref[column], tile)
    return tile


def fold(rows):
    total = jnp.zeros((8, LANES), F32)
    for r in range(rows.shape[0] // 8):
        for l in range(rows.shape[1] // LANES):
            total = total + rows[8 * r : 8 * r + 8, LANES * l : LANES * l + LANES]
    return total


def aligned(start, size):
    return pl.ds(pl.multiple_of(start, size), size)


def greet(axes):
    barrier = pltpu.get_barrier_semaphore()
    for axis, size in axes:
        me = lax.axis_index(axis)

        @pl.loop(1, size)
        def _(step):
            peer = lax.rem(me + step, size)
            pl.semaphore_signal(barrier, inc=1, device_id={axis: peer}, device_id_type=MESH)

    return barrier


def main_kernel(
    groups, parts, places, batch, challenge_ref, x_hbm, multiplicity_hbm, index_hbm, high_hbm, low_hbm,
    coset_hbm, own_ref, carry_ref,
    x_ref, multiplicity_ref, index_ref, high_ref, low_ref, coset_ref, moments_ref, local_ref, sums_ref, table_ref,
    partial_ref, send_ref, gathered_ref, edge_send, edge_recv, pieces_ref, note_ref, notes_ref, entry_ref, entries_ref,
    x_sem, load_sem, table_sem, store_sem, send_sem, recv_sem, edge_send_sem, edge_recv_sem,
    piece_send, piece_recv, note_send, note_recv, entry_send, entry_recv,
):
    me = lax.axis_index("rows")
    part = lax.axis_index("cols")
    rows = x_hbm.shape[1]
    leaves = rows // LEAF
    parents = leaves // RADIX
    tops = parents // RADIX
    span = LEAF * RADIX
    quarter_rows = rows // parts
    inner = pl.ds(LEAF, rows)

    def weights(name, first=0, last=None):
        start, stop = places[name]
        at = slice(start + first, stop if last is None else start + last)
        return high_ref[at, :], low_ref[at, :]

    early = places["up"][1]
    late = high_ref.shape[0] - early
    load_x = pltpu.make_async_copy(x_hbm, x_ref.at[:, inner], x_sem)
    loads = []
    for k, at in enumerate((pl.ds(0, early), pl.ds(early, late))):
        loads.append(
            [
                pltpu.make_async_copy(high_hbm.at[at], high_ref.at[at], load_sem.at[2 * k]),
                pltpu.make_async_copy(low_hbm.at[at], low_ref.at[at], load_sem.at[2 * k + 1]),
            ]
        )

    def table_loads(k):
        at = aligned(k * 2 * quarter_rows, 2 * quarter_rows)
        return (
            pltpu.make_async_copy(multiplicity_hbm.at[:, at], multiplicity_ref.at[:, at], table_sem.at[0, k]),
            pltpu.make_async_copy(index_hbm.at[:, at], index_ref.at[:, at], table_sem.at[1, k]),
        )

    for load in loads[0]:
        load.start()
    load_x.start()
    for k in range(parts):
        for load in table_loads(k):
            load.start()
    for load in loads[1]:
        load.start()
    barrier = greet((("rows", groups), ("cols", parts)))
    for load in loads[0]:
        load.wait()
    load_x.wait()

    own_group = lax.broadcasted_iota(jnp.int32, (LEAF, WIDE), 1) // NODES
    p2m = weights("p2m")
    total = jnp.zeros((8 * parents, WIDE), F32)
    for pair in range(RADIX // 2):
        start = LEAF + 2 * LEAF * pair
        left = jnp.concatenate(
            [x_ref[:, span * p + start : span * p + start + 2 * LEAF] for p in range(parents)], axis=0
        )
        right = [
            jnp.concatenate(
                [jnp.where(own_group == 2 * pair + k, piece, jnp.zeros_like(piece)) for k in range(2)], axis=0
            )
            for piece in p2m
        ]
        total = total + dot_pieces(two(left), right)
    moments_ref[...] = total
    up = weights("up")
    copies = dot_pieces(two(total), up)
    middle = [gather_children(copies[128 * g : 128 * g + 128]) for g in range(tops)]
    high = dot_pieces(two(jnp.concatenate(middle, axis=0)), [piece[:, :LANES] for piece in up])
    group = lax.broadcasted_iota(jnp.int32, (8, LANES), 1) // NODES
    packed = high[0:8]
    for g in range(1, tops):
        packed = jnp.where(group % tops == g, high[8 * g : 8 * g + 8], packed)
    send_ref[...] = packed
    edge_send[0, :, 0:LEAF] = x_ref[:, rows : rows + LEAF]
    edge_send[0, :, LEAF : LEAF + WIDE] = total[8 * (parents - 1) : 8 * parents]
    edge_send[0, :, LEAF + WIDE :] = middle[tops - 1]
    edge_send[1, :, 0:LEAF] = x_ref[:, LEAF : 2 * LEAF]
    edge_send[1, :, LEAF : LEAF + WIDE] = total[0:8]
    edge_send[1, :, LEAF + WIDE :] = middle[0]

    pl.semaphore_wait(barrier, groups + parts - 2)

    def edge(k):
        peer = lax.rem(me + (1 if k == 0 else groups - 1), groups)
        return pltpu.make_async_remote_copy(
            src_ref=edge_send.at[k], dst_ref=edge_recv.at[k], send_sem=edge_send_sem.at[k],
            recv_sem=edge_recv_sem.at[k], device_id={"rows": peer}, device_id_type=MESH,
        )

    def message(step):
        peer = lax.rem(me + groups - step, groups)
        return pltpu.make_async_remote_copy(
            src_ref=send_ref, dst_ref=gathered_ref.at[step], send_sem=send_sem.at[step],
            recv_sem=recv_sem.at[step], device_id={"rows": peer}, device_id_type=MESH,
        )

    @pl.loop(1, groups)
    def _(step):
        message(step).start()

    edge(0).start()
    edge(1).start()

    weight = challenge_tile(challenge_ref)
    per_part = leaves // parts // 8

    @pl.loop(0, parts)
    def _(k):
        for load in table_loads(k):
            load.wait()

        @pl.loop(0, per_part)
        def _(j):
            block = k * per_part + j
            out = aligned(8 * block, 8)
            tiles = [[], []]
            for tile in range(16):
                at = aligned((16 * block + tile) * LANES, LANES)
                value = (index_ref[:, at].astype(F32) - TABLE_ROWS / 2) * (8.0 / TABLE_ROWS)
                tiles[tile % 2].append(multiplicity_ref[:, at].astype(F32) * invert(weight + value * value))
            table_ref[out, 0:LANES] = column_sums(tiles[0])
            table_ref[out, LANES:] = column_sums(tiles[1])
            terms = []
            for tile in range(8):
                value = x_ref[:, aligned((8 * block + tile + 1) * LANES, LANES)]
                terms.append(invert(weight + value * value))
            sums_ref[out, 0:LANES] = column_sums(terms)

    for load in loads[1]:
        load.wait()
    gathered_ref[0] = send_ref[...]

    @pl.loop(1, groups)
    def _(step):
        message(step).wait()

    edge(0).wait()
    edge(1).wait()
    x_ref[:, 0:LEAF] = edge_recv[0, :, 0:LEAF]
    x_ref[:, rows + LEAF :] = edge_recv[1, :, 0:LEAF]
    per_tile = LANES // (tops * NODES)
    pieces = []
    for k in range(groups // per_tile):
        tile = gathered_ref[per_tile * k]
        for place in range(1, per_tile):
            tile = jnp.where(group // tops == place, gathered_ref[per_tile * k + place], tile)
        pieces.append(tile)
    top_local = dot_pieces(
        two(jnp.concatenate(pieces, axis=1)), [piece[:, :LANES] for piece in weights("top")]
    )
    top_pair = two(top_local)
    line = [edge_recv[0, :, LEAF + WIDE :]] + middle + [edge_recv[1, :, LEAF + WIDE :]]
    left = jnp.concatenate([jnp.concatenate(line[g : g + 3], axis=1) for g in range(tops)], axis=0)
    middle_local = dot_pieces(two(left), weights("far1"))
    expanded = []
    for g in range(tops):
        from_top = dot_pieces(top_pair, weights("top_down", LANES * g, LANES * g + LANES))
        expanded += spread(middle_local[8 * g : 8 * g + 8] + from_top, NODES)
    local = dot_pieces(two(jnp.concatenate(expanded, axis=0)), weights("down"))
    moments = moments_ref[...]
    before = jnp.concatenate([edge_recv[0, :, LEAF : LEAF + WIDE], moments[:-8]], axis=0)
    after = jnp.concatenate([moments[8:], edge_recv[1, :, LEAF : LEAF + WIDE]], axis=0)
    for k, source in enumerate((before, moments, after)):
        local = local + dot_pieces(two(source), weights("far0", k * WIDE, k * WIDE + WIDE))
    local_ref[...] = local

    def piece(step):
        peer = lax.rem(part + 1 + step, parts)
        at = aligned(peer * (leaves // parts), leaves // parts)
        return pltpu.make_async_remote_copy(
            src_ref=partial_ref.at[at], dst_ref=pieces_ref.at[step], send_sem=piece_send.at[step],
            recv_sem=piece_recv.at[step], device_id={"cols": peer}, device_id_type=MESH,
        )

    def store(step):
        at = aligned(lax.rem(part + 1 + step, parts) * quarter_rows, quarter_rows)
        return pltpu.make_async_copy(coset_ref.at[:, at], coset_hbm.at[:, at], store_sem.at[step])

    @pl.loop(0, parts)
    def _(step):
        quarter = lax.rem(part + 1 + step, parts)

        @pl.loop(0, parents // parts // batch)
        def _(chunk):
            first = quarter * (parents // parts) + chunk * batch
            start = first * span
            count = batch * RADIX
            tiles = [x_ref[:, aligned(start + LEAF * j, LEAF)] for j in range(count + 2)]
            sources = [jnp.concatenate(tiles[k : k + count : 2], axis=0) for k in range(4)]
            expanded = []
            for p in range(batch):
                expanded += spread(local_ref[aligned(8 * (first + p), 8), :], 2 * NODES)
            sources.append(jnp.concatenate(expanded, axis=0))
            pairs = [two(source) for source in sources]
            left = [jnp.concatenate([pair[k] for pair in pairs], axis=1) for k in range(2)]
            result = dot_pieces(left, weights("out"))
            terms = []
            for j in range(count // 2):
                both = result[8 * j : 8 * j + 8]
                coset_ref[:, aligned(start + 2 * LEAF * j, 2 * LEAF)] = both
                for half in range(2):
                    value = both[:, LANES * half : LANES * half + LANES]
                    terms.append(invert(weight + value * value))
            for j in range(count // 8):
                sums_ref[aligned(first * RADIX + 8 * j, 8), LANES:] = column_sums(terms[8 * j : 8 * j + 8])

        at = aligned(quarter * (leaves // parts), leaves // parts)
        partial_ref[at, :] = dot_exact(sums_ref[at, :], weights("weave")[0]) - table_ref[at, :]
        note_ref[quarter] = fold(partial_ref[at, :])
        store(step).start()

        @pl.when(step < parts - 1)
        def _():
            piece(step).start()

    totals = [note_ref[p] for p in range(parts)]
    entry_ref[0] = (totals[0] + totals[1]) + (totals[2] + totals[3])

    def note(step):
        peer = lax.rem(me + groups - step, groups)
        return pltpu.make_async_remote_copy(
            src_ref=entry_ref.at[0], dst_ref=notes_ref.at[step], send_sem=note_send.at[step],
            recv_sem=note_recv.at[step], device_id={"rows": peer}, device_id_type=MESH,
        )

    def entry(step):
        peer = lax.rem(part + parts - step, parts)
        return pltpu.make_async_remote_copy(
            src_ref=entry_ref.at[1 + peer], dst_ref=entries_ref.at[step], send_sem=entry_send.at[step],
            recv_sem=entry_recv.at[step], device_id={"cols": peer}, device_id_type=MESH,
        )

    @pl.loop(1, groups)
    def _(step):
        note(step).start()

    @pl.loop(0, parts - 1)
    def _(step):
        piece(step).wait()

    own = partial_ref[aligned(part * (leaves // parts), leaves // parts), :]
    for step in range(parts - 1):
        own = own + pieces_ref[step]
    own_ref[...] = own

    @pl.loop(0, parts)
    def _(step):
        store(step).wait()

    @pl.loop(1, groups)
    def _(step):
        note(step).wait()

    entering = jnp.zeros((8, LANES), F32)
    for step in range(1, groups):
        entering = entering + jnp.where(me + step >= groups, notes_ref[step], 0.0)
    for p in range(parts):
        entry_ref[1 + p] = entering
        entering = entering + totals[p]

    @pl.loop(1, parts)
    def _(step):
        entry(step).start()

    @pl.loop(1, parts)
    def _(step):
        entry(step).wait()

    carry = entry_ref[1 + part]
    for step in range(1, parts):
        carry = carry + entries_ref[step]
    carry_ref[...] = carry


def output_kernel(
    scale, x_ref, coset_ref, own_ref, carry_ref, lane_ref, row_ref, extended_ref, fraction_ref, running_ref
):
    lane = lax.broadcasted_iota(jnp.int32, (8, LANES), 1)
    even = lane % 2 == 0
    for tile in range(x_ref.shape[1] // LANES):
        at = slice(tile * LANES, (tile + 1) * LANES)
        values = (x_ref[:, at], coset_ref[:, at])
        for half in range(2):
            place = lane // 2 + half * (LANES // 2)
            sides = [jnp.take_along_axis(value, place, axis=1) for value in values]
            out = (2 * tile + half) * LANES
            extended_ref[:, out : out + LANES] = jnp.where(even, sides[0], sides[1])

    @pl.when(pl.program_id(0) == 0)
    def _():
        own = own_ref[...]
        size = own.shape[0]
        within = dot_exact(own, lane_ref[...])
        ends = jnp.broadcast_to(within[:, WIDE - 1 :], (size, LANES))
        high, low = two(ends)
        rest = (ends - high.astype(F32) - low.astype(F32)).astype(BF16)
        before = dot16(row_ref[...], rest) + dot16(row_ref[...], low) + dot16(row_ref[...], high)
        before = before + jnp.sum(carry_ref[...])
        for half in range(2):
            at = slice(half * LANES, (half + 1) * LANES)
            out = pl.ds(half, size, stride=2)
            fraction_ref[out, :] = own[:, at]
            running_ref[out, :] = (within[:, at] + before) * scale


def local(groups, parts, trace_values, challenges, multiplicity, table_index):
    columns, rows = trace_values.shape
    total = groups * rows
    (high, low), places = matrices(total, groups)
    leaves = rows // LEAF
    parents = leaves // RADIX
    vmem = pl.BlockSpec(memory_space=pltpu.VMEM)
    smem = pl.BlockSpec(memory_space=pltpu.SMEM)
    hbm = pl.BlockSpec(memory_space=pl.ANY)
    dma = pltpu.SemaphoreType.DMA
    size = leaves // parts
    tile = lambda *lead: pltpu.VMEM(lead + (columns, LANES), F32)
    coset, own, carry = pl.pallas_call(
        functools.partial(main_kernel, groups, parts, places, BATCH),
        out_shape=(
            jax.ShapeDtypeStruct((columns, rows), F32),
            jax.ShapeDtypeStruct((size, WIDE), F32),
            jax.ShapeDtypeStruct((columns, LANES), F32),
        ),
        in_specs=[smem] + [hbm] * 5,
        out_specs=(hbm, vmem, vmem),
        scratch_shapes=[
            pltpu.VMEM((columns, rows + 2 * LEAF), F32),
            pltpu.VMEM((columns, 2 * rows), jnp.int32),
            pltpu.VMEM((columns, 2 * rows), jnp.int32),
            pltpu.VMEM(high.shape, BF16),
            pltpu.VMEM(high.shape, BF16),
            pltpu.VMEM((columns, rows), F32),
            pltpu.VMEM((columns * parents, WIDE), F32),
            pltpu.VMEM((columns * parents, WIDE), F32),
            pltpu.VMEM((leaves, WIDE), F32),
            pltpu.VMEM((leaves, WIDE), F32),
            pltpu.VMEM((leaves, WIDE), F32),
            tile(),
            tile(groups),
            pltpu.VMEM((2, columns, LEAF + 2 * WIDE), F32),
            pltpu.VMEM((2, columns, LEAF + 2 * WIDE), F32),
            pltpu.VMEM((parts - 1, size, WIDE), F32),
            tile(parts),
            tile(groups),
            tile(1 + parts),
            tile(parts),
            dma, dma((4,)), dma((2, parts)), dma((parts,)),
            dma((groups,)), dma((groups,)), dma((2,)), dma((2,)),
            dma((parts,)), dma((parts,)), dma((groups,)), dma((groups,)), dma((parts,)), dma((parts,)),
        ],
        compiler_params=pltpu.CompilerParams(
            collective_id=0, has_side_effects=True, vmem_limit_bytes=56 * 2**20
        ),
        name="main",
    )(challenges, trace_values, multiplicity, table_index, high, low)
    steps = 8
    whole = lambda *shape: pl.BlockSpec(shape, lambda i: (0,) * len(shape))
    lane_sum = np.triu(np.ones((WIDE, WIDE))).astype(ml_dtypes.bfloat16)
    row_sum = np.tril(np.ones((size, size)), -1).astype(ml_dtypes.bfloat16)
    flat = jax.ShapeDtypeStruct((2 * size, LANES), F32)
    extended, fraction, running = pl.pallas_call(
        functools.partial(output_kernel, 1.0 / (2 * total)),
        grid=(steps,),
        out_shape=(jax.ShapeDtypeStruct((columns, 2 * rows), F32), flat, flat),
        in_specs=[
            pl.BlockSpec((columns, rows // steps), lambda i: (0, i)),
            pl.BlockSpec((columns, rows // steps), lambda i: (0, i)),
            whole(size, WIDE),
            whole(columns, LANES),
            whole(WIDE, WIDE),
            whole(size, size),
        ],
        out_specs=(
            pl.BlockSpec((columns, 2 * rows // steps), lambda i: (0, i)),
            whole(2 * size, LANES),
            whole(2 * size, LANES),
        ),
        compiler_params=pltpu.CompilerParams(vmem_limit_bytes=32 * 2**20),
        name="weave",
    )(trace_values, coset, own, carry, lane_sum, row_sum)
    return extended, fraction.reshape(-1), running.reshape(-1)


def solution(mesh):
    return jax.shard_map(
        functools.partial(local, mesh.shape["rows"], mesh.shape["cols"]),
        mesh=mesh,
        in_specs=(P("cols", "rows"), P("cols"), P("cols", "rows"), P("cols", "rows")),
        out_specs=(P("cols", "rows"), P(("rows", "cols")), P(("rows", "cols"))),
        check_vma=False,
    )
```

time: 55 us -> 47.5 us (0.86)
  the two profiles are of different devices: /device:TPU:1 before, /device:TPU:0 now
where the time goes in v1:
time: 47.5 us; the launch traced here: 47.3 us
  Pallas kernels  43.4 us (91%)
  local copies, waits for them, and re-layouts  3.19 us (7%)
  between operations  0.7 us (1%)
    pallas_call x1, Pallas kernels, local(): pl.pallas_call(functools.partial(main_kernel, groups, parts, places, BATC...  36.3 us
    pallas_call x1, Pallas kernels, local(): pl.pallas_call(functools.partial(output_kernel, 1.0 / (2 * total)), grid=...  7.1 us
    unnamed x12, local copies, waits for them, and re-layouts  3.19 us

profile of v1, /device:TPU:0, one launch (start us, length us, event | category | flops | bytes accessed | tf_op | source)
XLA Modules:
  0.0 47.3 jit_solution(1157474552931009579)
XLA Ops:
  0.6 0.0 copy-start.2
  0.6 0.0 copy-start.4
  0.7 0.0 copy-start
  0.7 36.3 %main.1 = (f32[8,65536]{1,0:T(8,128)}, f32[128,256]{1,0:T(8,128)}, f32[8,128]{1,0:T(8,128)}) custom-call(f32[8]{0:T(128)} %challenge_ref.1, f32[8,65536]{1,0:T(8,128)} %x_ref.1, s32[8,131072]{1,0:T(8,128)} %multiplicity_hbm.1, s32[8,131072]{1,0:T(8,128)} %index_hbm.1, bf16[4224,256]{1,0:T(8,128)(2,1)} %constant.8.clone.high_hbm, ...), custom_call_target="tpu_custom_call" | custom-call | tf_op jit(solution)/shard_map/main/pallas_call | solution.py:530
  37.0 0.0 copy-done.2
  37.0 0.0 copy-done.4
  37.0 0.0 copy-done
  37.0 0.0 copy-start.1
  37.0 1.6 %copy-done.1 = f32[8,65536]{1,0:T(8,128)S(1)} copy-done((f32[8,65536]{1,0:T(8,128)S(1)}, f32[8,65536]{1,0:T(8,128)}, u32[]{:S(2)}) %copy-start.1) | copy-done | bytes 2097176
  38.6 0.0 copy-start.3
  38.6 0.9 %copy-done.3 = f32[128,256]{1,0:T(8,128)S(1)} copy-done((f32[128,256]{1,0:T(8,128)S(1)}, f32[128,256]{1,0:T(8,128)}, u32[]{:S(2)}) %copy-start.3) | copy-done | bytes 131096
  39.5 0.0 copy-start.5
  39.5 0.7 %copy-done.5 = f32[8,128]{1,0:T(8,128)S(1)} copy-done((f32[8,128]{1,0:T(8,128)S(1)}, f32[8,128]{1,0:T(8,128)}, u32[]{:S(2)}) %copy-start.5) | copy-done | bytes 4120
  40.2 7.1 %weave.1 = (f32[8,131072]{1,0:T(8,128)}, f32[256,128]{1,0:T(8,128)}, f32[256,128]{1,0:T(8,128)}) custom-call(f32[8,65536]{1,0:T(8,128)S(1)} %copy-done, f32[8,65536]{1,0:T(8,128)S(1)} %copy-done.1, f32[128,256]{1,0:T(8,128)S(1)} %copy-done.3, f32[8,128]{1,0:T(8,128)S(1)} %copy-done.5, bf16[256,256]{1,0:T(8,128)(2,1)S(1)} %copy-done.2, ...), custom_call_target="tpu_custom_call" | custom-call | tf_op jit(solution)/shard_map/weave/pallas_call | solution.py:574
Async XLA Ops:
  0.6 36.4 %copy-start.2 = (bf16[256,256]{1,0:T(8,128)(2,1)S(1)}, bf16[256,256]{1,0:T(8,128)(2,1)}, u32[]{:S(2)}) copy-start(bf16[256,256]{1,0:T(8,128)(2,1)} %constant.10.clone.lane_ref) | copy-start | bytes 393220
  0.6 36.4 %copy-start.4 = (bf16[128,128]{1,0:T(8,128)(2,1)S(1)}, bf16[128,128]{1,0:T(8,128)(2,1)}, u32[]{:S(2)}) copy-start(bf16[128,128]{1,0:T(8,128)(2,1)} %constant.11.clone.row_ref) | copy-start | bytes 98308
  0.7 36.4 %copy-start = (f32[8,65536]{1,0:T(8,128)S(1)}, f32[8,65536]{1,0:T(8,128)}, u32[]{:S(2)}) copy-start(f32[8,65536]{1,0:T(8,128)} %x_ref.1) | copy-start | bytes 6291460
  37.0 1.6 %copy-start.1 = (f32[8,65536]{1,0:T(8,128)S(1)}, f32[8,65536]{1,0:T(8,128)}, u32[]{:S(2)}) copy-start(f32[8,65536]{1,0:T(8,128)} %get-tuple-element.9.coset_ref) | copy-start | bytes 6291460
  38.6 0.9 %copy-start.3 = (f32[128,256]{1,0:T(8,128)S(1)}, f32[128,256]{1,0:T(8,128)}, u32[]{:S(2)}) copy-start(f32[128,256]{1,0:T(8,128)} %get-tuple-element.10.own_ref) | copy-start | bytes 393220
  39.5 0.7 %copy-start.5 = (f32[8,128]{1,0:T(8,128)S(1)}, f32[8,128]{1,0:T(8,128)}, u32[]{:S(2)}) copy-start(f32[8,128]{1,0:T(8,128)} %get-tuple-element.11.carry_ref) | copy-start | bytes 12292

commit v2 on v1

--- a/solution.py
+++ b/solution.py
@@ -17,6 +17,10 @@
 LANES = 128
 WIDE = RADIX * NODES
 BATCH = 4
+CHUNKS = 4
+STEPS = ((2, 0), (2, 1), (1, 1), (3, 0), (1, 0), (3, 1), (0, 0), (0, 1))
+QUARTERS = sum(quarter * 4**step for step, (quarter, _) in enumerate(STEPS))
+HALVES = sum(half * 2**step for step, (_, half) in enumerate(STEPS))
 MESH = pl.DeviceIdType.MESH
 F32 = jnp.float32
 BF16 = jnp.bfloat16
@@ -127,13 +131,17 @@
 
 
 def dot_pieces(left, right):
-    return dot16(left[1], right[0]) + dot16(left[0], right[1]) + dot16(left[0], right[0])
+    rows = left[0].shape[0]
+    both = dot16(jnp.concatenate(left, axis=0), right[0])
+    return both[rows:] + dot16(left[0], right[1]) + both[:rows]
 
 
 def dot_exact(left, right):
+    rows = left.shape[0]
     high, low = two(left)
     rest = (left - high.astype(F32) - low.astype(F32)).astype(BF16)
-    return dot16(rest, right) + dot16(low, right) + dot16(high, right)
+    pieces = dot16(jnp.concatenate([rest, low, high], axis=0), right)
+    return pieces[:rows] + pieces[rows : 2 * rows] + pieces[2 * rows :]
 
 
 def spread(local, span):
@@ -248,15 +256,15 @@
     for load in loads[0]:
         load.start()
     load_x.start()
+    barrier = greet((("rows", groups), ("cols", parts)))
+    for load in loads[0]:
+        load.wait()
+    load_x.wait()
     for k in range(parts):
         for load in table_loads(k):
             load.start()
     for load in loads[1]:
         load.start()
-    barrier = greet((("rows", groups), ("cols", parts)))
-    for load in loads[0]:
-        load.wait()
-    load_x.wait()
 
     own_group = lax.broadcasted_iota(jnp.int32, (LEAF, WIDE), 1) // NODES
     p2m = weights("p2m")
@@ -306,12 +314,12 @@
             recv_sem=recv_sem.at[step], device_id={"rows": peer}, device_id_type=MESH,
         )
 
-    @pl.loop(1, groups)
-    def _(step):
-        message(step).start()
-
     edge(0).start()
     edge(1).start()
+
+    @pl.loop(1, groups)
+    def _(step):
+        message(step).start()
 
     weight = challenge_tile(challenge_ref)
     per_part = leaves // parts // 8
@@ -340,16 +348,30 @@
 
     for load in loads[1]:
         load.wait()
+    moments = moments_ref[...]
+    blank = jnp.zeros((8, WIDE), F32)
+    far0 = [weights("far0", k * WIDE, k * WIDE + WIDE) for k in range(3)]
+    far1 = [weights("far1", k * WIDE, k * WIDE + WIDE) for k in range(3)]
+    local = dot_pieces(two(moments), far0[1])
+    local = local + dot_pieces(two(jnp.concatenate([blank, moments[:-8]], axis=0)), far0[0])
+    local_ref[...] = local + dot_pieces(two(jnp.concatenate([moments[8:], blank], axis=0)), far0[2])
+    line = [blank] + middle + [blank]
+    left = jnp.concatenate([jnp.concatenate(line[g : g + 3], axis=1) for g in range(tops)], axis=0)
+    inner_local = dot_pieces(two(left), weights("far1"))
     gathered_ref[0] = send_ref[...]
-
-    @pl.loop(1, groups)
-    def _(step):
-        message(step).wait()
 
     edge(0).wait()
     edge(1).wait()
     x_ref[:, 0:LEAF] = edge_recv[0, :, 0:LEAF]
     x_ref[:, rows + LEAF :] = edge_recv[1, :, 0:LEAF]
+    for k, at in ((0, slice(0, 8)), (1, slice(8 * parents - 8, 8 * parents))):
+        local_ref[at, :] = local_ref[at, :] + dot_pieces(two(edge_recv[k, :, LEAF : LEAF + WIDE]), far0[2 * k])
+    edges = [dot_pieces(two(edge_recv[k, :, LEAF + WIDE :]), far1[2 * k]) for k in range(2)]
+
+    @pl.loop(1, groups)
+    def _(step):
+        message(step).wait()
+
     per_tile = LANES // (tops * NODES)
     pieces = []
     for k in range(groups // per_tile):
@@ -361,40 +383,52 @@
         two(jnp.concatenate(pieces, axis=1)), [piece[:, :LANES] for piece in weights("top")]
     )
     top_pair = two(top_local)
-    line = [edge_recv[0, :, LEAF + WIDE :]] + middle + [edge_recv[1, :, LEAF + WIDE :]]
-    left = jnp.concatenate([jnp.concatenate(line[g : g + 3], axis=1) for g in range(tops)], axis=0)
-    middle_local = dot_pieces(two(left), weights("far1"))
     expanded = []
     for g in range(tops):
-        from_top = dot_pieces(top_pair, weights("top_down", LANES * g, LANES * g + LANES))
-        expanded += spread(middle_local[8 * g : 8 * g + 8] + from_top, NODES)
-    local = dot_pieces(two(jnp.concatenate(expanded, axis=0)), weights("down"))
-    moments = moments_ref[...]
-    before = jnp.concatenate([edge_recv[0, :, LEAF : LEAF + WIDE], moments[:-8]], axis=0)
-    after = jnp.concatenate([moments[8:], edge_recv[1, :, LEAF : LEAF + WIDE]], axis=0)
-    for k, source in enumerate((before, moments, after)):
-        local = local + dot_pieces(two(source), weights("far0", k * WIDE, k * WIDE + WIDE))
-    local_ref[...] = local
-
-    def piece(step):
-        peer = lax.rem(part + 1 + step, parts)
-        at = aligned(peer * (leaves // parts), leaves // parts)
+        here = dot_pieces(top_pair, weights("top_down", LANES * g, LANES * g + LANES))
+        here = here + inner_local[8 * g : 8 * g + 8]
+        if g == 0:
+            here = here + edges[0]
+        if g == tops - 1:
+            here = here + edges[1]
+        expanded += spread(here, NODES)
+    local_ref[...] = local_ref[...] + dot_pieces(two(jnp.concatenate(expanded, axis=0)), weights("down"))
+
+    half_leaves = leaves // parts // 2
+    half_rows = quarter_rows // 2
+    before_me = lax.rem(part + parts - 1, parts)
+    after_me = lax.rem(part + 1, parts)
+
+    def half_at(quarter, half):
+        return aligned((2 * quarter + half) * half_leaves, half_leaves)
+
+    def ship(slot, source, peer):
         return pltpu.make_async_remote_copy(
-            src_ref=partial_ref.at[at], dst_ref=pieces_ref.at[step], send_sem=piece_send.at[step],
-            recv_sem=piece_recv.at[step], device_id={"cols": peer}, device_id_type=MESH,
-        )
-
-    def store(step):
-        at = aligned(lax.rem(part + 1 + step, parts) * quarter_rows, quarter_rows)
+            src_ref=partial_ref.at[source], dst_ref=pieces_ref.at[slot], send_sem=piece_send.at[slot],
+            recv_sem=piece_recv.at[slot], device_id={"cols": peer}, device_id_type=MESH,
+        )
+
+    opposite = lax.rem(part + 2, parts)
+    ships = (
+        ship(0, half_at(opposite, 0), after_me),
+        ship(1, half_at(opposite, 1), before_me),
+        ship(2, half_at(after_me, 1), after_me),
+        ship(3, half_at(before_me, 0), before_me),
+        ship(4, half_at(after_me, 0), after_me),
+        ship(5, half_at(before_me, 1), before_me),
+    )
+
+    def store(step, at):
         return pltpu.make_async_copy(coset_ref.at[:, at], coset_hbm.at[:, at], store_sem.at[step])
 
-    @pl.loop(0, parts)
-    def _(step):
-        quarter = lax.rem(part + 1 + step, parts)
-
-        @pl.loop(0, parents // parts // batch)
+    @pl.loop(0, 2 * parts)
+    def _(step):
+        quarter = lax.rem(part + lax.rem(lax.shift_right_logical(QUARTERS, 2 * step), 4), parts)
+        half = 2 * quarter + lax.rem(lax.shift_right_logical(HALVES, step), 2)
+
+        @pl.loop(0, half_leaves // RADIX // batch)
         def _(chunk):
-            first = quarter * (parents // parts) + chunk * batch
+            first = half * (half_leaves // RADIX) + chunk * batch
             start = first * span
             count = batch * RADIX
             tiles = [x_ref[:, aligned(start + LEAF * j, LEAF)] for j in range(count + 2)]
@@ -410,22 +444,27 @@
             for j in range(count // 2):
                 both = result[8 * j : 8 * j + 8]
                 coset_ref[:, aligned(start + 2 * LEAF * j, 2 * LEAF)] = both
-                for half in range(2):
-                    value = both[:, LANES * half : LANES * half + LANES]
+                for side in range(2):
+                    value = both[:, LANES * side : LANES * side + LANES]
                     terms.append(invert(weight + value * value))
             for j in range(count // 8):
                 sums_ref[aligned(first * RADIX + 8 * j, 8), LANES:] = column_sums(terms[8 * j : 8 * j + 8])
 
-        at = aligned(quarter * (leaves // parts), leaves // parts)
-        partial_ref[at, :] = dot_exact(sums_ref[at, :], weights("weave")[0]) - table_ref[at, :]
-        note_ref[quarter] = fold(partial_ref[at, :])
-        store(step).start()
-
-        @pl.when(step < parts - 1)
-        def _():
-            piece(step).start()
-
-    totals = [note_ref[p] for p in range(parts)]
+        at = aligned(half * half_leaves, half_leaves)
+        partial = dot_exact(sums_ref[at, :], weights("weave")[0]) - table_ref[at, :]
+        note_ref[half] = fold(partial)
+        partial_ref[at, :] = partial
+        store(step, aligned(half * half_rows, half_rows)).start()
+        for k in range(6):
+
+            @pl.when(step == k)
+            def _(k=k):
+                if k >= 4:
+                    ships[k - 4].wait_recv()
+                    partial_ref[at, :] = partial_ref[at, :] + pieces_ref[k - 4]
+                ships[k].start()
+
+    totals = [note_ref[2 * p] + note_ref[2 * p + 1] for p in range(parts)]
     entry_ref[0] = (totals[0] + totals[1]) + (totals[2] + totals[3])
 
     def note(step):
@@ -446,18 +485,17 @@
     def _(step):
         note(step).start()
 
-    @pl.loop(0, parts - 1)
-    def _(step):
-        piece(step).wait()
-
-    own = partial_ref[aligned(part * (leaves // parts), leaves // parts), :]
-    for step in range(parts - 1):
-        own = own + pieces_ref[step]
-    own_ref[...] = own
-
-    @pl.loop(0, parts)
-    def _(step):
-        store(step).wait()
+    for k in range(2):
+        ships[k].wait_send()
+    for k in range(2, 6):
+        ships[k].wait()
+    for half, slots in ((0, (3, 4)), (1, (2, 5))):
+        own = partial_ref[half_at(part, half), :]
+        own_ref[half * half_leaves : (half + 1) * half_leaves, :] = own + pieces_ref[slots[0]] + pieces_ref[slots[1]]
+
+    @pl.loop(0, 2 * parts)
+    def _(step):
+        store(step, aligned(step * half_rows, half_rows)).wait()
 
     @pl.loop(1, groups)
     def _(step):
@@ -485,34 +523,80 @@
 
 
 def output_kernel(
-    scale, x_ref, coset_ref, own_ref, carry_ref, lane_ref, row_ref, extended_ref, fraction_ref, running_ref
+    scale, x_hbm, coset_hbm, own_hbm, carry_hbm, weave_hbm, lane_hbm, row_hbm, extended_hbm, fraction_hbm, running_hbm,
+    x_ref, coset_ref, own_ref, carry_ref, weave_ref, lane_ref, row_ref, extended_ref, fraction_ref, running_ref,
+    load_sem, x_sem, coset_sem, out_sem, store_sem,
 ):
-    lane = lax.broadcasted_iota(jnp.int32, (8, LANES), 1)
-    even = lane % 2 == 0
-    for tile in range(x_ref.shape[1] // LANES):
-        at = slice(tile * LANES, (tile + 1) * LANES)
-        values = (x_ref[:, at], coset_ref[:, at])
-        for half in range(2):
-            place = lane // 2 + half * (LANES // 2)
-            sides = [jnp.take_along_axis(value, place, axis=1) for value in values]
-            out = (2 * tile + half) * LANES
-            extended_ref[:, out : out + LANES] = jnp.where(even, sides[0], sides[1])
-
-    @pl.when(pl.program_id(0) == 0)
-    def _():
-        own = own_ref[...]
-        size = own.shape[0]
-        within = dot_exact(own, lane_ref[...])
-        ends = jnp.broadcast_to(within[:, WIDE - 1 :], (size, LANES))
-        high, low = two(ends)
-        rest = (ends - high.astype(F32) - low.astype(F32)).astype(BF16)
-        before = dot16(row_ref[...], rest) + dot16(row_ref[...], low) + dot16(row_ref[...], high)
-        before = before + jnp.sum(carry_ref[...])
-        for half in range(2):
-            at = slice(half * LANES, (half + 1) * LANES)
-            out = pl.ds(half, size, stride=2)
-            fraction_ref[out, :] = own[:, at]
-            running_ref[out, :] = (within[:, at] + before) * scale
+    rows = x_ref.shape[1]
+    chunks = x_sem.shape[0]
+    size = rows // chunks
+    small = (
+        (weave_hbm, weave_ref), (own_hbm, own_ref), (carry_hbm, carry_ref), (lane_hbm, lane_ref), (row_hbm, row_ref),
+    )
+    loads = [pltpu.make_async_copy(*pair, load_sem.at[k]) for k, pair in enumerate(small)]
+
+    def rows_in(k):
+        at = aligned(k * size, size)
+        return (
+            pltpu.make_async_copy(x_hbm.at[:, at], x_ref.at[:, at], x_sem.at[k]),
+            pltpu.make_async_copy(coset_hbm.at[:, at], coset_ref.at[:, at], coset_sem.at[k]),
+        )
+
+    def rows_out(k):
+        at = aligned(2 * k * size, 2 * size)
+        return pltpu.make_async_copy(extended_ref.at[:, at], extended_hbm.at[:, at], out_sem.at[k])
+
+    loads[0].start()
+    for k in range(chunks):
+        for load in rows_in(k):
+            load.start()
+    for load in loads[1:]:
+        load.start()
+    loads[0].wait()
+
+    @pl.loop(0, chunks)
+    def _(k):
+        for load in rows_in(k):
+            load.wait()
+        count = size // LANES
+        slices = [aligned(k * size + tile * LANES, LANES) for tile in range(count)]
+        own = jnp.concatenate([x_ref[:, at] for at in slices], axis=0)
+        between = jnp.concatenate([coset_ref[:, at] for at in slices], axis=0)
+        high, low = two(own)
+        rest = (own - high.astype(F32) - low.astype(F32)).astype(BF16)
+        both = dot16(jnp.concatenate([rest, low, high, *two(between)], axis=1), weave_ref[...])
+        for tile in range(count):
+            extended_ref[:, aligned(2 * k * size + tile * WIDE, WIDE)] = both[8 * tile : 8 * tile + 8]
+        rows_out(k).start()
+
+    for load in loads[1:]:
+        load.wait()
+    own = own_ref[...]
+    size_own = own.shape[0]
+    within = dot_exact(own, lane_ref[...])
+    ends = jnp.broadcast_to(within[:, WIDE - 1 :], (size_own, LANES))
+    high, low = two(ends)
+    rest = (ends - high.astype(F32) - low.astype(F32)).astype(BF16)
+    before = dot16(row_ref[...], rest) + dot16(row_ref[...], low) + dot16(row_ref[...], high)
+    before = before + jnp.sum(carry_ref[...])
+    for half in range(2):
+        at = slice(half * LANES, (half + 1) * LANES)
+        out = pl.ds(half, size_own, stride=2)
+        fraction_ref[out, :] = own[:, at]
+        running_ref[out, :] = (within[:, at] + before) * scale
+    stores = [
+        pltpu.make_async_copy(fraction_ref, fraction_hbm, store_sem.at[0]),
+        pltpu.make_async_copy(running_ref, running_hbm, store_sem.at[1]),
+    ]
+    for store in stores:
+        store.start()
+
+    @pl.loop(0, chunks)
+    def _(k):
+        rows_out(k).wait()
+
+    for store in stores:
+        store.wait()
 
 
 def local(groups, parts, trace_values, challenges, multiplicity, table_index):
@@ -552,45 +636,45 @@
             tile(groups),
             pltpu.VMEM((2, columns, LEAF + 2 * WIDE), F32),
             pltpu.VMEM((2, columns, LEAF + 2 * WIDE), F32),
-            pltpu.VMEM((parts - 1, size, WIDE), F32),
-            tile(parts),
+            pltpu.VMEM((6, size // 2, WIDE), F32),
+            tile(2 * parts),
             tile(groups),
             tile(1 + parts),
             tile(parts),
-            dma, dma((4,)), dma((2, parts)), dma((parts,)),
+            dma, dma((4,)), dma((2, parts)), dma((2 * parts,)),
             dma((groups,)), dma((groups,)), dma((2,)), dma((2,)),
-            dma((parts,)), dma((parts,)), dma((groups,)), dma((groups,)), dma((parts,)), dma((parts,)),
+            dma((6,)), dma((6,)), dma((groups,)), dma((groups,)), dma((parts,)), dma((parts,)),
         ],
         compiler_params=pltpu.CompilerParams(
             collective_id=0, has_side_effects=True, vmem_limit_bytes=56 * 2**20
         ),
         name="main",
     )(challenges, trace_values, multiplicity, table_index, high, low)
-    steps = 8
-    whole = lambda *shape: pl.BlockSpec(shape, lambda i: (0,) * len(shape))
+    weave_rows = high[slice(*places["weave"])].reshape(2, LEAF, WIDE)[np.array((0, 0, 0, 1, 1))].reshape(-1, WIDE)
     lane_sum = np.triu(np.ones((WIDE, WIDE))).astype(ml_dtypes.bfloat16)
     row_sum = np.tril(np.ones((size, size)), -1).astype(ml_dtypes.bfloat16)
     flat = jax.ShapeDtypeStruct((2 * size, LANES), F32)
     extended, fraction, running = pl.pallas_call(
         functools.partial(output_kernel, 1.0 / (2 * total)),
-        grid=(steps,),
         out_shape=(jax.ShapeDtypeStruct((columns, 2 * rows), F32), flat, flat),
-        in_specs=[
-            pl.BlockSpec((columns, rows // steps), lambda i: (0, i)),
-            pl.BlockSpec((columns, rows // steps), lambda i: (0, i)),
-            whole(size, WIDE),
-            whole(columns, LANES),
-            whole(WIDE, WIDE),
-            whole(size, size),
+        in_specs=[hbm] * 7,
+        out_specs=(hbm, hbm, hbm),
+        scratch_shapes=[
+            pltpu.VMEM((columns, rows), F32),
+            pltpu.VMEM((columns, rows), F32),
+            pltpu.VMEM((size, WIDE), F32),
+            tile(),
+            pltpu.VMEM((5 * LEAF, WIDE), BF16),
+            pltpu.VMEM((WIDE, WIDE), BF16),
+            pltpu.VMEM((size, size), BF16),
+            pltpu.VMEM((columns, 2 * rows), F32),
+            pltpu.VMEM((2 * size, LANES), F32),
+            pltpu.VMEM((2 * size, LANES), F32),
+            dma((5,)), dma((CHUNKS,)), dma((CHUNKS,)), dma((CHUNKS,)), dma((2,)),
         ],
-        out_specs=(
-            pl.BlockSpec((columns, 2 * rows // steps), lambda i: (0, i)),
-            whole(2 * size, LANES),
-            whole(2 * size, LANES),
-        ),
-        compiler_params=pltpu.CompilerParams(vmem_limit_bytes=32 * 2**20),
+        compiler_params=pltpu.CompilerParams(vmem_limit_bytes=60 * 2**20),
         name="weave",
-    )(trace_values, coset, own, carry, lane_sum, row_sum)
+    )(trace_values, coset, own, carry, weave_rows, lane_sum, row_sum)
     return extended, fraction.reshape(-1), running.reshape(-1)
 
 

time: 47.5 us -> 39.7 us (0.84)
  Pallas kernels: 43.4 us -> 38.9 us
  local copies, waits for them, and re-layouts: 3.19 us -> 0 us
    unnamed x12 -> x0, local copies, waits for them, and re-layouts: 3.19 us -> none
    pallas_call x1, Pallas kernels: 36.3 us -> 33.9 us  [local(): pl.pallas_call(functools.partial(main_kernel, groups, parts, places, BATC...]
    pallas_call x1, Pallas kernels: 7.1 us -> 4.98 us  [local(): pl.pallas_call(functools.partial(output_kernel, 1.0 / (2 * total)), out_s...]
where the time goes in v2:
time: 39.7 us; the launch traced here: 39.5 us
  Pallas kernels  38.9 us (98%)
  between operations  0.64 us (2%)
    pallas_call x1, Pallas kernels, local(): pl.pallas_call(functools.partial(main_kernel, groups, parts, places, BATC...  33.9 us
    pallas_call x1, Pallas kernels, local(): pl.pallas_call(functools.partial(output_kernel, 1.0 / (2 * total)), out_s...  4.98 us

profile of v2, /device:TPU:0, one launch (start us, length us, event | category | flops | bytes accessed | tf_op | source)
XLA Modules:
  0.0 39.5 jit_solution(11239720409185880945)
XLA Ops:
  0.6 33.9 %main.1 = (f32[8,65536]{1,0:T(8,128)}, f32[128,256]{1,0:T(8,128)}, f32[8,128]{1,0:T(8,128)}) custom-call(f32[8]{0:T(128)} %challenge_ref.1, f32[8,65536]{1,0:T(8,128)} %x_hbm.3, s32[8,131072]{1,0:T(8,128)} %multiplicity_hbm.1, s32[8,131072]{1,0:T(8,128)} %index_hbm.1, bf16[4224,256]{1,0:T(8,128)(2,1)} %constant.10.clone.high_hbm, ...), custom_call_target="tpu_custom_call" | custom-call | tf_op jit(solution)/shard_map/main/pallas_call | solution.py:614
  34.5 5.0 %weave.1 = (f32[8,131072]{1,0:T(8,128)}, f32[256,128]{1,0:T(8,128)}, f32[256,128]{1,0:T(8,128)}) custom-call(f32[8,65536]{1,0:T(8,128)} %x_hbm.3, f32[8,65536]{1,0:T(8,128)} %get-tuple-element.9.coset_hbm, f32[128,256]{1,0:T(8,128)} %get-tuple-element.10.own_hbm, f32[8,128]{1,0:T(8,128)} %get-tuple-element.11.carry_hbm, ...), custom_call_target="tpu_custom_call" | custom-call | tf_op jit(solution)/shard_map/weave/pallas_call | solution.py:657

commit v3 on v2

--- a/solution.py
+++ b/solution.py
@@ -18,6 +18,7 @@
 WIDE = RADIX * NODES
 BATCH = 4
 CHUNKS = 4
+FAR_FIRST = 2 + 1 * 4 + 3 * 16 + 0 * 64
 STEPS = ((2, 0), (2, 1), (1, 1), (3, 0), (1, 0), (3, 1), (0, 0), (0, 1))
 QUARTERS = sum(quarter * 4**step for step, (quarter, _) in enumerate(STEPS))
 HALVES = sum(half * 2**step for step, (_, half) in enumerate(STEPS))
@@ -113,6 +114,7 @@
         down=np.tile(c2p.T, (LANES // NODES, 1)),
         out=np.concatenate([near, child_out.reshape(LANES, WIDE)]),
         weave=weave.reshape(2 * LEAF, WIDE),
+        part=weave.reshape(2 * LEAF, WIDE).T,
     )
     places, start = {}, 0
     for name, part in parts.items():
@@ -174,8 +176,7 @@
 
 
 def invert(value):
-    guess = pl.reciprocal(value, approx=True)
-    return guess * (2.0 - value * guess)
+    return pl.reciprocal(value, approx=True)
 
 
 def challenge_tile(challenge_ref):
@@ -186,16 +187,15 @@
     return tile
 
 
-def fold(rows):
-    total = jnp.zeros((8, LANES), F32)
-    for r in range(rows.shape[0] // 8):
-        for l in range(rows.shape[1] // LANES):
-            total = total + rows[8 * r : 8 * r + 8, LANES * l : LANES * l + LANES]
-    return total
-
-
 def aligned(start, size):
     return pl.ds(pl.multiple_of(start, size), size)
+
+
+def row_peer(me, step):
+    across = lax.rem(me // 8 + lax.rem(lax.shift_right_logical(FAR_FIRST, 2 * (step // 8)), 4), 4)
+    along = lax.rem(me // 2 + lax.rem(lax.shift_right_logical(FAR_FIRST, 2 * lax.rem(step // 2, 4)), 4), 4)
+    core = lax.rem(me + 1 + step, 2)
+    return 8 * across + 2 * along + core
 
 
 def greet(axes):
@@ -213,10 +213,10 @@
 
 def main_kernel(
     groups, parts, places, batch, challenge_ref, x_hbm, multiplicity_hbm, index_hbm, high_hbm, low_hbm,
-    coset_hbm, own_ref, carry_ref,
-    x_ref, multiplicity_ref, index_ref, high_ref, low_ref, coset_ref, moments_ref, local_ref, sums_ref, table_ref,
-    partial_ref, send_ref, gathered_ref, edge_send, edge_recv, pieces_ref, note_ref, notes_ref, entry_ref, entries_ref,
-    x_sem, load_sem, table_sem, store_sem, send_sem, recv_sem, edge_send_sem, edge_recv_sem,
+    coset_hbm, own_hbm, carry_hbm,
+    x_ref, multiplicity_ref, index_ref, high_ref, low_ref, coset_ref, moments_ref, local_ref, own_ref, table_ref,
+    partial_ref, gathered_ref, edge_send, edge_recv, pieces_ref, note_ref, notes_ref, entry_ref,
+    x_sem, load_sem, table_sem, store_sem, own_sem, send_sem, recv_sem, edge_send_sem, edge_recv_sem,
     piece_send, piece_recv, note_send, note_recv, entry_send, entry_recv,
 ):
     me = lax.axis_index("rows")
@@ -290,7 +290,7 @@
     packed = high[0:8]
     for g in range(1, tops):
         packed = jnp.where(group % tops == g, high[8 * g : 8 * g + 8], packed)
-    send_ref[...] = packed
+    gathered_ref[me] = packed
     edge_send[0, :, 0:LEAF] = x_ref[:, rows : rows + LEAF]
     edge_send[0, :, LEAF : LEAF + WIDE] = total[8 * (parents - 1) : 8 * parents]
     edge_send[0, :, LEAF + WIDE :] = middle[tops - 1]
@@ -308,20 +308,24 @@
         )
 
     def message(step):
-        peer = lax.rem(me + groups - step, groups)
         return pltpu.make_async_remote_copy(
-            src_ref=send_ref, dst_ref=gathered_ref.at[step], send_sem=send_sem.at[step],
-            recv_sem=recv_sem.at[step], device_id={"rows": peer}, device_id_type=MESH,
-        )
+            src_ref=gathered_ref.at[me], dst_ref=gathered_ref.at[me], send_sem=send_sem, recv_sem=recv_sem,
+            device_id={"rows": row_peer(me, step)}, device_id_type=MESH,
+        )
+
+    def all_peers(slots_ref, semaphore):
+        there = slots_ref.at[pl.ds(0, groups - 1)]
+        return pltpu.make_async_copy(there, there, semaphore)
 
     edge(0).start()
     edge(1).start()
 
-    @pl.loop(1, groups)
+    @pl.loop(0, groups - 1)
     def _(step):
         message(step).start()
 
     weight = challenge_tile(challenge_ref)
+    table_weight = weight * (TABLE_ROWS / 8.0) ** 2
     per_part = leaves // parts // 8
 
     @pl.loop(0, parts)
@@ -336,18 +340,22 @@
             tiles = [[], []]
             for tile in range(16):
                 at = aligned((16 * block + tile) * LANES, LANES)
-                value = (index_ref[:, at].astype(F32) - TABLE_ROWS / 2) * (8.0 / TABLE_ROWS)
-                tiles[tile % 2].append(multiplicity_ref[:, at].astype(F32) * invert(weight + value * value))
-            table_ref[out, 0:LANES] = column_sums(tiles[0])
-            table_ref[out, LANES:] = column_sums(tiles[1])
+                value = index_ref[:, at].astype(F32) - TABLE_ROWS / 2
+                tiles[tile % 2].append(multiplicity_ref[:, at].astype(F32) * invert(table_weight + value * value))
+            table_ref[out, 0:LANES] = column_sums(tiles[0]) * (TABLE_ROWS / 8.0) ** 2
+            table_ref[out, LANES:] = column_sums(tiles[1]) * (TABLE_ROWS / 8.0) ** 2
             terms = []
             for tile in range(8):
                 value = x_ref[:, aligned((8 * block + tile + 1) * LANES, LANES)]
                 terms.append(invert(weight + value * value))
-            sums_ref[out, 0:LANES] = column_sums(terms)
+            partial_ref[out, 0:LANES] = column_sums(terms)
 
     for load in loads[1]:
         load.wait()
+    shares = dot_exact(table_ref[...], weights("part")[0])
+    partial_ref[:, 0:LANES] = partial_ref[:, 0:LANES] - shares[:, 0:LANES]
+    table_ref[:, LANES:] = shares[:, LANES:]
+
     moments = moments_ref[...]
     blank = jnp.zeros((8, WIDE), F32)
     far0 = [weights("far0", k * WIDE, k * WIDE + WIDE) for k in range(3)]
@@ -358,7 +366,6 @@
     line = [blank] + middle + [blank]
     left = jnp.concatenate([jnp.concatenate(line[g : g + 3], axis=1) for g in range(tops)], axis=0)
     inner_local = dot_pieces(two(left), weights("far1"))
-    gathered_ref[0] = send_ref[...]
 
     edge(0).wait()
     edge(1).wait()
@@ -368,16 +375,15 @@
         local_ref[at, :] = local_ref[at, :] + dot_pieces(two(edge_recv[k, :, LEAF : LEAF + WIDE]), far0[2 * k])
     edges = [dot_pieces(two(edge_recv[k, :, LEAF + WIDE :]), far1[2 * k]) for k in range(2)]
 
-    @pl.loop(1, groups)
-    def _(step):
-        message(step).wait()
+    all_peers(gathered_ref, recv_sem).wait()
 
     per_tile = LANES // (tops * NODES)
     pieces = []
     for k in range(groups // per_tile):
-        tile = gathered_ref[per_tile * k]
+        tile = gathered_ref[lax.rem(me + per_tile * k, groups)]
         for place in range(1, per_tile):
-            tile = jnp.where(group // tops == place, gathered_ref[per_tile * k + place], tile)
+            there = gathered_ref[lax.rem(me + per_tile * k + place, groups)]
+            tile = jnp.where(group // tops == place, there, tile)
         pieces.append(tile)
     top_local = dot_pieces(
         two(jnp.concatenate(pieces, axis=1)), [piece[:, :LANES] for piece in weights("top")]
@@ -440,7 +446,7 @@
             pairs = [two(source) for source in sources]
             left = [jnp.concatenate([pair[k] for pair in pairs], axis=1) for k in range(2)]
             result = dot_pieces(left, weights("out"))
-            terms = []
+            terms, total = [], jnp.zeros((8, LANES), F32)
             for j in range(count // 2):
                 both = result[8 * j : 8 * j + 8]
                 coset_ref[:, aligned(start + 2 * LEAF * j, 2 * LEAF)] = both
@@ -448,43 +454,60 @@
                     value = both[:, LANES * side : LANES * side + LANES]
                     terms.append(invert(weight + value * value))
             for j in range(count // 8):
-                sums_ref[aligned(first * RADIX + 8 * j, 8), LANES:] = column_sums(terms[8 * j : 8 * j + 8])
+                at = aligned(first * RADIX + 8 * j, 8)
+                odd = column_sums(terms[8 * j : 8 * j + 8]) - table_ref[at, LANES:]
+                partial_ref[at, LANES:] = odd
+                total = total + (odd + partial_ref[at, 0:LANES])
+            note_ref[half] = total
 
         at = aligned(half * half_leaves, half_leaves)
-        partial = dot_exact(sums_ref[at, :], weights("weave")[0]) - table_ref[at, :]
-        note_ref[half] = fold(partial)
-        partial_ref[at, :] = partial
         store(step, aligned(half * half_rows, half_rows)).start()
-        for k in range(6):
+        for k in range(4):
 
             @pl.when(step == k)
             def _(k=k):
-                if k >= 4:
-                    ships[k - 4].wait_recv()
-                    partial_ref[at, :] = partial_ref[at, :] + pieces_ref[k - 4]
                 ships[k].start()
 
     totals = [note_ref[2 * p] + note_ref[2 * p + 1] for p in range(parts)]
-    entry_ref[0] = (totals[0] + totals[1]) + (totals[2] + totals[3])
+    notes_ref[me] = (totals[0] + totals[1]) + (totals[2] + totals[3])
 
     def note(step):
-        peer = lax.rem(me + groups - step, groups)
         return pltpu.make_async_remote_copy(
-            src_ref=entry_ref.at[0], dst_ref=notes_ref.at[step], send_sem=note_send.at[step],
-            recv_sem=note_recv.at[step], device_id={"rows": peer}, device_id_type=MESH,
+            src_ref=notes_ref.at[me], dst_ref=notes_ref.at[me], send_sem=note_send, recv_sem=note_recv,
+            device_id={"rows": row_peer(me, step)}, device_id_type=MESH,
         )
 
     def entry(step):
         peer = lax.rem(part + parts - step, parts)
         return pltpu.make_async_remote_copy(
-            src_ref=entry_ref.at[1 + peer], dst_ref=entries_ref.at[step], send_sem=entry_send.at[step],
+            src_ref=entry_ref.at[peer], dst_ref=carry_hbm.at[step], send_sem=entry_send.at[step],
             recv_sem=entry_recv.at[step], device_id={"cols": peer}, device_id_type=MESH,
         )
 
-    @pl.loop(1, groups)
+    @pl.loop(0, groups - 1)
     def _(step):
         note(step).start()
 
+    for k in (4, 5):
+        ships[k - 4].wait_recv()
+        at = half_at((after_me, before_me)[k - 4], k - 4)
+        partial_ref[at, :] = partial_ref[at, :] + pieces_ref[k - 4]
+        ships[k].start()
+
+    all_peers(notes_ref, note_recv).wait()
+    entering = jnp.zeros((8, LANES), F32)
+    for k in range(groups):
+        entering = entering + jnp.where(k < me, notes_ref[k], 0.0)
+    for p in range(parts):
+        entry_ref[p] = entering
+        entering = entering + totals[p]
+
+    @pl.loop(1, parts)
+    def _(step):
+        entry(step).start()
+
+    own_entry = pltpu.make_async_copy(entry_ref.at[part], carry_hbm.at[0], own_sem.at[1])
+    own_entry.start()
     for k in range(2):
         ships[k].wait_send()
     for k in range(2, 6):
@@ -492,46 +515,35 @@
     for half, slots in ((0, (3, 4)), (1, (2, 5))):
         own = partial_ref[half_at(part, half), :]
         own_ref[half * half_leaves : (half + 1) * half_leaves, :] = own + pieces_ref[slots[0]] + pieces_ref[slots[1]]
+    own_store = pltpu.make_async_copy(own_ref, own_hbm, own_sem.at[0])
+    own_store.start()
 
     @pl.loop(0, 2 * parts)
     def _(step):
         store(step, aligned(step * half_rows, half_rows)).wait()
 
-    @pl.loop(1, groups)
-    def _(step):
-        note(step).wait()
-
-    entering = jnp.zeros((8, LANES), F32)
-    for step in range(1, groups):
-        entering = entering + jnp.where(me + step >= groups, notes_ref[step], 0.0)
-    for p in range(parts):
-        entry_ref[1 + p] = entering
-        entering = entering + totals[p]
-
-    @pl.loop(1, parts)
-    def _(step):
-        entry(step).start()
+    own_store.wait()
+    own_entry.wait()
 
     @pl.loop(1, parts)
     def _(step):
         entry(step).wait()
 
-    carry = entry_ref[1 + part]
-    for step in range(1, parts):
-        carry = carry + entries_ref[step]
-    carry_ref[...] = carry
+    all_peers(gathered_ref, send_sem).wait()
+    all_peers(notes_ref, note_send).wait()
 
 
 def output_kernel(
-    scale, x_hbm, coset_hbm, own_hbm, carry_hbm, weave_hbm, lane_hbm, row_hbm, extended_hbm, fraction_hbm, running_hbm,
-    x_ref, coset_ref, own_ref, carry_ref, weave_ref, lane_ref, row_ref, extended_ref, fraction_ref, running_ref,
+    scale, x_hbm, coset_hbm, own_hbm, carry_hbm, weave_hbm, order_hbm, lane_hbm, row_hbm, extended_hbm, fraction_hbm, running_hbm,
+    x_ref, coset_ref, own_ref, carry_ref, weave_ref, order_ref, lane_ref, row_ref, extended_ref, fraction_ref, running_ref,
     load_sem, x_sem, coset_sem, out_sem, store_sem,
 ):
     rows = x_ref.shape[1]
     chunks = x_sem.shape[0]
     size = rows // chunks
     small = (
-        (weave_hbm, weave_ref), (own_hbm, own_ref), (carry_hbm, carry_ref), (lane_hbm, lane_ref), (row_hbm, row_ref),
+        (weave_hbm, weave_ref), (own_hbm, own_ref), (carry_hbm, carry_ref), (order_hbm, order_ref),
+        (lane_hbm, lane_ref), (row_hbm, row_ref),
     )
     loads = [pltpu.make_async_copy(*pair, load_sem.at[k]) for k, pair in enumerate(small)]
 
@@ -573,6 +585,7 @@
         load.wait()
     own = own_ref[...]
     size_own = own.shape[0]
+    fraction = dot_exact(own, order_ref[...])
     within = dot_exact(own, lane_ref[...])
     ends = jnp.broadcast_to(within[:, WIDE - 1 :], (size_own, LANES))
     high, low = two(ends)
@@ -582,7 +595,7 @@
     for half in range(2):
         at = slice(half * LANES, (half + 1) * LANES)
         out = pl.ds(half, size_own, stride=2)
-        fraction_ref[out, :] = own[:, at]
+        fraction_ref[out, :] = fraction[:, at]
         running_ref[out, :] = (within[:, at] + before) * scale
     stores = [
         pltpu.make_async_copy(fraction_ref, fraction_hbm, store_sem.at[0]),
@@ -605,7 +618,6 @@
     (high, low), places = matrices(total, groups)
     leaves = rows // LEAF
     parents = leaves // RADIX
-    vmem = pl.BlockSpec(memory_space=pltpu.VMEM)
     smem = pl.BlockSpec(memory_space=pltpu.SMEM)
     hbm = pl.BlockSpec(memory_space=pl.ANY)
     dma = pltpu.SemaphoreType.DMA
@@ -616,10 +628,10 @@
         out_shape=(
             jax.ShapeDtypeStruct((columns, rows), F32),
             jax.ShapeDtypeStruct((size, WIDE), F32),
-            jax.ShapeDtypeStruct((columns, LANES), F32),
+            jax.ShapeDtypeStruct((parts, columns, LANES), F32),
         ),
         in_specs=[smem] + [hbm] * 5,
-        out_specs=(hbm, vmem, vmem),
+        out_specs=(hbm, hbm, hbm),
         scratch_shapes=[
             pltpu.VMEM((columns, rows + 2 * LEAF), F32),
             pltpu.VMEM((columns, 2 * rows), jnp.int32),
@@ -629,52 +641,52 @@
             pltpu.VMEM((columns, rows), F32),
             pltpu.VMEM((columns * parents, WIDE), F32),
             pltpu.VMEM((columns * parents, WIDE), F32),
+            pltpu.VMEM((size, WIDE), F32),
             pltpu.VMEM((leaves, WIDE), F32),
             pltpu.VMEM((leaves, WIDE), F32),
-            pltpu.VMEM((leaves, WIDE), F32),
-            tile(),
             tile(groups),
             pltpu.VMEM((2, columns, LEAF + 2 * WIDE), F32),
             pltpu.VMEM((2, columns, LEAF + 2 * WIDE), F32),
             pltpu.VMEM((6, size // 2, WIDE), F32),
             tile(2 * parts),
             tile(groups),
-            tile(1 + parts),
             tile(parts),
-            dma, dma((4,)), dma((2, parts)), dma((2 * parts,)),
-            dma((groups,)), dma((groups,)), dma((2,)), dma((2,)),
-            dma((6,)), dma((6,)), dma((groups,)), dma((groups,)), dma((parts,)), dma((parts,)),
+            dma, dma((4,)), dma((2, parts)), dma((2 * parts,)), dma((2,)),
+            dma, dma, dma((2,)), dma((2,)),
+            dma((6,)), dma((6,)), dma, dma, dma((parts,)), dma((parts,)),
         ],
         compiler_params=pltpu.CompilerParams(
             collective_id=0, has_side_effects=True, vmem_limit_bytes=56 * 2**20
         ),
         name="main",
     )(challenges, trace_values, multiplicity, table_index, high, low)
-    weave_rows = high[slice(*places["weave"])].reshape(2, LEAF, WIDE)[np.array((0, 0, 0, 1, 1))].reshape(-1, WIDE)
-    lane_sum = np.triu(np.ones((WIDE, WIDE))).astype(ml_dtypes.bfloat16)
+    order = high[slice(*places["weave"])]
+    weave_rows = order.reshape(2, LEAF, WIDE)[np.array((0, 0, 0, 1, 1))].reshape(-1, WIDE)
+    lane_sum = (order.astype(np.float32) @ np.triu(np.ones((WIDE, WIDE), np.float32))).astype(ml_dtypes.bfloat16)
     row_sum = np.tril(np.ones((size, size)), -1).astype(ml_dtypes.bfloat16)
     flat = jax.ShapeDtypeStruct((2 * size, LANES), F32)
     extended, fraction, running = pl.pallas_call(
         functools.partial(output_kernel, 1.0 / (2 * total)),
         out_shape=(jax.ShapeDtypeStruct((columns, 2 * rows), F32), flat, flat),
-        in_specs=[hbm] * 7,
+        in_specs=[hbm] * 8,
         out_specs=(hbm, hbm, hbm),
         scratch_shapes=[
             pltpu.VMEM((columns, rows), F32),
             pltpu.VMEM((columns, rows), F32),
             pltpu.VMEM((size, WIDE), F32),
-            tile(),
+            tile(parts),
             pltpu.VMEM((5 * LEAF, WIDE), BF16),
+            pltpu.VMEM((WIDE, WIDE), BF16),
             pltpu.VMEM((WIDE, WIDE), BF16),
             pltpu.VMEM((size, size), BF16),
             pltpu.VMEM((columns, 2 * rows), F32),
             pltpu.VMEM((2 * size, LANES), F32),
             pltpu.VMEM((2 * size, LANES), F32),
-            dma((5,)), dma((CHUNKS,)), dma((CHUNKS,)), dma((CHUNKS,)), dma((2,)),
+            dma((6,)), dma((CHUNKS,)), dma((CHUNKS,)), dma((CHUNKS,)), dma((2,)),
         ],
         compiler_params=pltpu.CompilerParams(vmem_limit_bytes=60 * 2**20),
         name="weave",
-    )(trace_values, coset, own, carry, weave_rows, lane_sum, row_sum)
+    )(trace_values, coset, own, carry, weave_rows, order, lane_sum, row_sum)
     return extended, fraction.reshape(-1), running.reshape(-1)
 
 

time: 39.7 us -> 35.5 us (0.89)
  Pallas kernels: 38.9 us -> 34.7 us
    pallas_call x1, Pallas kernels: 33.9 us -> 29.6 us  [local(): pl.pallas_call(functools.partial(main_kernel, groups, parts, places, BATC...]
where the time goes in v3:
time: 35.5 us; the launch traced here: 35.3 us
  Pallas kernels  34.7 us (98%)
  between operations  0.64 us (2%)
    pallas_call x1, Pallas kernels, local(): pl.pallas_call(functools.partial(main_kernel, groups, parts, places, BATC...  29.6 us
    pallas_call x1, Pallas kernels, local(): pl.pallas_call(functools.partial(output_kernel, 1.0 / (2 * total)), out_s...  5.07 us

profile of v3, /device:TPU:0, one launch (start us, length us, event | category | flops | bytes accessed | tf_op | source)
XLA Modules:
  0.0 35.3 jit_solution(16821481056200316243)
XLA Ops:
  0.6 29.6 %main.1 = (f32[8,65536]{1,0:T(8,128)}, f32[128,256]{1,0:T(8,128)}, f32[4,8,128]{2,1,0:T(8,128)}) custom-call(f32[8]{0:T(128)} %challenge_ref.1, f32[8,65536]{1,0:T(8,128)} %x_hbm.3, s32[8,131072]{1,0:T(8,128)} %multiplicity_hbm.1, s32[8,131072]{1,0:T(8,128)} %index_hbm.1, bf16[4480,256]{1,0:T(8,128)(2,1)} %constant.12.clone.high_hbm, ...), custom_call_target="tpu_custom_call" | custom-call | tf_op jit(solution)/shard_map/main/pallas_call | solution.py:626
  30.3 5.1 %weave.1 = (f32[8,131072]{1,0:T(8,128)}, f32[256,128]{1,0:T(8,128)}, f32[256,128]{1,0:T(8,128)}) custom-call(f32[8,65536]{1,0:T(8,128)} %x_hbm.3, f32[8,65536]{1,0:T(8,128)} %get-tuple-element.9.coset_hbm, f32[128,256]{1,0:T(8,128)} %get-tuple-element.10.own_hbm, f32[4,8,128]{2,1,0:T(8,128)} %get-tuple-element.11.carry_hbm, ...), custom_call_target="tpu_custom_call" | custom-call | tf_op jit(solution)/shard_map/weave/pallas_call | solution.py:668

commit v4 on v3

--- a/solution.py
+++ b/solution.py
@@ -16,7 +16,8 @@
 RADIX = 16
 LANES = 128
 WIDE = RADIX * NODES
-BATCH = 4
+TABLE_BATCH = 2
+TABLE_AFTER = 2
 CHUNKS = 4
 FAR_FIRST = 2 + 1 * 4 + 3 * 16 + 0 * 64
 STEPS = ((2, 0), (2, 1), (1, 1), (3, 0), (1, 0), (3, 1), (0, 0), (0, 1))
@@ -115,12 +116,15 @@
         out=np.concatenate([near, child_out.reshape(LANES, WIDE)]),
         weave=weave.reshape(2 * LEAF, WIDE),
         part=weave.reshape(2 * LEAF, WIDE).T,
+        lane=weave.reshape(2 * LEAF, WIDE) @ np.triu(np.ones((WIDE, WIDE))),
+        row=np.tile(np.tril(np.ones((LANES, LANES)), -1), (1, 2)),
     )
     places, start = {}, 0
     for name, part in parts.items():
         places[name] = (start, start + part.shape[0])
         start += part.shape[0]
-    return split(np.concatenate(list(parts.values()))), places
+    high, low = split(np.concatenate(list(parts.values())))
+    return (high, low[: places["weave"][0]]), places
 
 
 def dot16(left, right):
@@ -212,9 +216,9 @@
 
 
 def main_kernel(
-    groups, parts, places, batch, challenge_ref, x_hbm, multiplicity_hbm, index_hbm, high_hbm, low_hbm,
-    coset_hbm, own_hbm, carry_hbm,
-    x_ref, multiplicity_ref, index_ref, high_ref, low_ref, coset_ref, moments_ref, local_ref, own_ref, table_ref,
+    groups, parts, scale, places, challenge_hbm, x_hbm, multiplicity_hbm, index_hbm, high_hbm, low_hbm,
+    extended_out, fraction_out, running_out, carry_out,
+    challenge_ref, x_ref, multiplicity_ref, index_ref, high_ref, low_ref, coset_ref, extended_ref, weave_ref, moments_ref, local_ref, fraction_ref, running_ref, table_ref,
     partial_ref, gathered_ref, edge_send, edge_recv, pieces_ref, note_ref, notes_ref, entry_ref,
     x_sem, load_sem, table_sem, store_sem, own_sem, send_sem, recv_sem, edge_send_sem, edge_recv_sem,
     piece_send, piece_recv, note_send, note_recv, entry_send, entry_recv,
@@ -227,24 +231,32 @@
     tops = parents // RADIX
     span = LEAF * RADIX
     quarter_rows = rows // parts
-    inner = pl.ds(LEAF, rows)
 
     def weights(name, first=0, last=None):
         start, stop = places[name]
         at = slice(start + first, stop if last is None else start + last)
         return high_ref[at, :], low_ref[at, :]
 
+    def ones(name):
+        return high_ref[slice(*places[name]), :]
+
     early = places["up"][1]
-    late = high_ref.shape[0] - early
-    load_x = pltpu.make_async_copy(x_hbm, x_ref.at[:, inner], x_sem)
+    load_x = [
+        pltpu.make_async_copy(
+            x_hbm.at[:, pl.ds(k * quarter_rows, quarter_rows)],
+            x_ref.at[:, pl.ds(LEAF + k * quarter_rows, quarter_rows)],
+            x_sem.at[k],
+        )
+        for k in range(parts)
+    ]
     loads = []
-    for k, at in enumerate((pl.ds(0, early), pl.ds(early, late))):
-        loads.append(
-            [
-                pltpu.make_async_copy(high_hbm.at[at], high_ref.at[at], load_sem.at[2 * k]),
-                pltpu.make_async_copy(low_hbm.at[at], low_ref.at[at], load_sem.at[2 * k + 1]),
-            ]
-        )
+    for k in range(2):
+        pair = []
+        for j, (source, target) in enumerate(((high_hbm, high_ref), (low_hbm, low_ref))):
+            at = pl.ds(early, target.shape[0] - early) if k else pl.ds(0, early)
+            pair.append(pltpu.make_async_copy(source.at[at], target.at[at], load_sem.at[2 * k + j]))
+        loads.append(pair)
+    load_challenges = pltpu.make_async_copy(challenge_hbm, challenge_ref, load_sem.at[4])
 
     def table_loads(k):
         at = aligned(k * 2 * quarter_rows, 2 * quarter_rows)
@@ -255,16 +267,20 @@
 
     for load in loads[0]:
         load.start()
-    load_x.start()
+    load_challenges.start()
+    for load in load_x:
+        load.start()
     barrier = greet((("rows", groups), ("cols", parts)))
     for load in loads[0]:
         load.wait()
-    load_x.wait()
     for k in range(parts):
-        for load in table_loads(k):
-            load.start()
-    for load in loads[1]:
-        load.start()
+        load_x[k].wait()
+        if k == TABLE_AFTER:
+            for j in range(parts):
+                for load in table_loads(j):
+                    load.start()
+            for load in loads[1]:
+                load.start()
 
     own_group = lax.broadcasted_iota(jnp.int32, (LEAF, WIDE), 1) // NODES
     p2m = weights("p2m")
@@ -324,57 +340,54 @@
     def _(step):
         message(step).start()
 
+    load_challenges.wait()
     weight = challenge_tile(challenge_ref)
     table_weight = weight * (TABLE_ROWS / 8.0) ** 2
     per_part = leaves // parts // 8
+
+    def table_block(block):
+        out = aligned(8 * block, 8)
+        tiles = [[], []]
+        for tile in range(16):
+            at = aligned((16 * block + tile) * LANES, LANES)
+            value = index_ref[:, at].astype(F32) - TABLE_ROWS / 2
+            tiles[tile % 2].append(multiplicity_ref[:, at].astype(F32) * invert(table_weight + value * value))
+        table_ref[out, 0:LANES] = column_sums(tiles[0]) * (TABLE_ROWS / 8.0) ** 2
+        table_ref[out, LANES:] = column_sums(tiles[1]) * (TABLE_ROWS / 8.0) ** 2
+        terms = []
+        for tile in range(8):
+            value = x_ref[:, aligned((8 * block + tile + 1) * LANES, LANES)]
+            terms.append(invert(weight + value * value))
+        partial_ref[out, 0:LANES] = column_sums(terms)
 
     @pl.loop(0, parts)
     def _(k):
         for load in table_loads(k):
             load.wait()
 
-        @pl.loop(0, per_part)
+        @pl.loop(0, per_part // TABLE_BATCH)
         def _(j):
-            block = k * per_part + j
-            out = aligned(8 * block, 8)
-            tiles = [[], []]
-            for tile in range(16):
-                at = aligned((16 * block + tile) * LANES, LANES)
-                value = index_ref[:, at].astype(F32) - TABLE_ROWS / 2
-                tiles[tile % 2].append(multiplicity_ref[:, at].astype(F32) * invert(table_weight + value * value))
-            table_ref[out, 0:LANES] = column_sums(tiles[0]) * (TABLE_ROWS / 8.0) ** 2
-            table_ref[out, LANES:] = column_sums(tiles[1]) * (TABLE_ROWS / 8.0) ** 2
-            terms = []
-            for tile in range(8):
-                value = x_ref[:, aligned((8 * block + tile + 1) * LANES, LANES)]
-                terms.append(invert(weight + value * value))
-            partial_ref[out, 0:LANES] = column_sums(terms)
+            for more in range(TABLE_BATCH):
+                table_block(k * per_part + j * TABLE_BATCH + more)
 
     for load in loads[1]:
         load.wait()
-    shares = dot_exact(table_ref[...], weights("part")[0])
+    shares = dot_exact(table_ref[...], ones("part"))
     partial_ref[:, 0:LANES] = partial_ref[:, 0:LANES] - shares[:, 0:LANES]
     table_ref[:, LANES:] = shares[:, LANES:]
 
     moments = moments_ref[...]
-    blank = jnp.zeros((8, WIDE), F32)
-    far0 = [weights("far0", k * WIDE, k * WIDE + WIDE) for k in range(3)]
-    far1 = [weights("far1", k * WIDE, k * WIDE + WIDE) for k in range(3)]
-    local = dot_pieces(two(moments), far0[1])
-    local = local + dot_pieces(two(jnp.concatenate([blank, moments[:-8]], axis=0)), far0[0])
-    local_ref[...] = local + dot_pieces(two(jnp.concatenate([moments[8:], blank], axis=0)), far0[2])
-    line = [blank] + middle + [blank]
-    left = jnp.concatenate([jnp.concatenate(line[g : g + 3], axis=1) for g in range(tops)], axis=0)
-    inner_local = dot_pieces(two(left), weights("far1"))
-
     edge(0).wait()
     edge(1).wait()
     x_ref[:, 0:LEAF] = edge_recv[0, :, 0:LEAF]
     x_ref[:, rows + LEAF :] = edge_recv[1, :, 0:LEAF]
-    for k, at in ((0, slice(0, 8)), (1, slice(8 * parents - 8, 8 * parents))):
-        local_ref[at, :] = local_ref[at, :] + dot_pieces(two(edge_recv[k, :, LEAF : LEAF + WIDE]), far0[2 * k])
-    edges = [dot_pieces(two(edge_recv[k, :, LEAF + WIDE :]), far1[2 * k]) for k in range(2)]
-
+    before = jnp.concatenate([edge_recv[0, :, LEAF : LEAF + WIDE], moments[:-8]], axis=0)
+    after = jnp.concatenate([moments[8:], edge_recv[1, :, LEAF : LEAF + WIDE]], axis=0)
+    left = jnp.concatenate([before, moments, after], axis=1)
+    local_ref[...] = dot_pieces(two(left), weights("far0"))
+    line = [edge_recv[0, :, LEAF + WIDE :]] + middle + [edge_recv[1, :, LEAF + WIDE :]]
+    left = jnp.concatenate([jnp.concatenate(line[g : g + 3], axis=1) for g in range(tops)], axis=0)
+    middle_local = dot_pieces(two(left), weights("far1"))
     all_peers(gathered_ref, recv_sem).wait()
 
     per_tile = LANES // (tops * NODES)
@@ -392,11 +405,7 @@
     expanded = []
     for g in range(tops):
         here = dot_pieces(top_pair, weights("top_down", LANES * g, LANES * g + LANES))
-        here = here + inner_local[8 * g : 8 * g + 8]
-        if g == 0:
-            here = here + edges[0]
-        if g == tops - 1:
-            here = here + edges[1]
+        here = here + middle_local[8 * g : 8 * g + 8]
         expanded += spread(here, NODES)
     local_ref[...] = local_ref[...] + dot_pieces(two(jnp.concatenate(expanded, axis=0)), weights("down"))
 
@@ -424,49 +433,51 @@
         ship(5, half_at(before_me, 1), before_me),
     )
 
-    def store(step, at):
-        return pltpu.make_async_copy(coset_ref.at[:, at], coset_hbm.at[:, at], store_sem.at[step])
-
-    @pl.loop(0, 2 * parts)
+    def half_of(step):
+        quarter = lax.rem(part + lax.rem(lax.shift_right_logical(QUARTERS, 2 * step), 4), parts)
+        return 2 * quarter + lax.rem(lax.shift_right_logical(HALVES, step), 2)
+
+    def product(half):
+        start = half * half_rows
+        tiles = [x_ref[:, aligned(start + LEAF * j, LEAF)] for j in range(half_leaves + 2)]
+        sources = [jnp.concatenate(tiles[k : k + half_leaves : 2], axis=0) for k in range(4)]
+        expanded = []
+        for p in range(half_leaves // RADIX):
+            expanded += spread(local_ref[aligned(8 * (half * (half_leaves // RADIX) + p), 8), :], 2 * NODES)
+        sources.append(jnp.concatenate(expanded, axis=0))
+        pairs = [two(source) for source in sources]
+        left = [jnp.concatenate([pair[k] for pair in pairs], axis=1) for k in range(2)]
+        result = dot_pieces(left, weights("out"))
+        for j in range(half_leaves // 2):
+            coset_ref[:, aligned(start + 2 * LEAF * j, 2 * LEAF)] = result[8 * j : 8 * j + 8]
+
+    def sums(half):
+        total = jnp.zeros((8, LANES), F32)
+        for j in range(half_leaves // 8):
+            terms = []
+            for k in range(8):
+                value = coset_ref[:, aligned(half * half_rows + LEAF * (8 * j + k), LEAF)]
+                terms.append(invert(weight + value * value))
+            at = aligned(half * half_leaves + 8 * j, 8)
+            odd = column_sums(terms) - table_ref[at, LANES:]
+            partial_ref[at, LANES:] = odd
+            total = total + (odd + partial_ref[at, 0:LANES])
+        note_ref[half] = total
+
+    product(half_of(0))
+
+    @pl.loop(1, 2 * parts)
     def _(step):
-        quarter = lax.rem(part + lax.rem(lax.shift_right_logical(QUARTERS, 2 * step), 4), parts)
-        half = 2 * quarter + lax.rem(lax.shift_right_logical(HALVES, step), 2)
-
-        @pl.loop(0, half_leaves // RADIX // batch)
-        def _(chunk):
-            first = half * (half_leaves // RADIX) + chunk * batch
-            start = first * span
-            count = batch * RADIX
-            tiles = [x_ref[:, aligned(start + LEAF * j, LEAF)] for j in range(count + 2)]
-            sources = [jnp.concatenate(tiles[k : k + count : 2], axis=0) for k in range(4)]
-            expanded = []
-            for p in range(batch):
-                expanded += spread(local_ref[aligned(8 * (first + p), 8), :], 2 * NODES)
-            sources.append(jnp.concatenate(expanded, axis=0))
-            pairs = [two(source) for source in sources]
-            left = [jnp.concatenate([pair[k] for pair in pairs], axis=1) for k in range(2)]
-            result = dot_pieces(left, weights("out"))
-            terms, total = [], jnp.zeros((8, LANES), F32)
-            for j in range(count // 2):
-                both = result[8 * j : 8 * j + 8]
-                coset_ref[:, aligned(start + 2 * LEAF * j, 2 * LEAF)] = both
-                for side in range(2):
-                    value = both[:, LANES * side : LANES * side + LANES]
-                    terms.append(invert(weight + value * value))
-            for j in range(count // 8):
-                at = aligned(first * RADIX + 8 * j, 8)
-                odd = column_sums(terms[8 * j : 8 * j + 8]) - table_ref[at, LANES:]
-                partial_ref[at, LANES:] = odd
-                total = total + (odd + partial_ref[at, 0:LANES])
-            note_ref[half] = total
-
-        at = aligned(half * half_leaves, half_leaves)
-        store(step, aligned(half * half_rows, half_rows)).start()
+        half = half_of(step - 1)
+        sums(half)
+        product(half_of(step))
         for k in range(4):
 
-            @pl.when(step == k)
+            @pl.when(step == k + 1)
             def _(k=k):
                 ships[k].start()
+
+    sums(half_of(2 * parts - 1))
 
     totals = [note_ref[2 * p] + note_ref[2 * p + 1] for p in range(parts)]
     notes_ref[me] = (totals[0] + totals[1]) + (totals[2] + totals[3])
@@ -480,7 +491,7 @@
     def entry(step):
         peer = lax.rem(part + parts - step, parts)
         return pltpu.make_async_remote_copy(
-            src_ref=entry_ref.at[peer], dst_ref=carry_hbm.at[step], send_sem=entry_send.at[step],
+            src_ref=entry_ref.at[peer], dst_ref=carry_out.at[step], send_sem=entry_send.at[step],
             recv_sem=entry_recv.at[step], device_id={"cols": peer}, device_id_type=MESH,
         )
 
@@ -493,6 +504,29 @@
         at = half_at((after_me, before_me)[k - 4], k - 4)
         partial_ref[at, :] = partial_ref[at, :] + pieces_ref[k - 4]
         ships[k].start()
+
+    size = rows // CHUNKS
+    weave = ones("weave")
+    for k in range(5):
+        weave_ref[LEAF * k : LEAF * k + LEAF, :] = weave[:LEAF] if k < 3 else weave[LEAF:]
+
+    def hand_over(k):
+        at = aligned(2 * k * size, 2 * size)
+        return pltpu.make_async_copy(extended_ref.at[:, at], extended_out.at[:, at], store_sem.at[k])
+
+    @pl.loop(0, CHUNKS)
+    def _(k):
+        count = size // LANES
+        trace = [x_ref[:, aligned(LEAF + k * size + tile * LANES, LANES)] for tile in range(count)]
+        trace = jnp.concatenate(trace, axis=0)
+        between = [coset_ref[:, aligned(k * size + tile * LANES, LANES)] for tile in range(count)]
+        between = jnp.concatenate(between, axis=0)
+        high, low = two(trace)
+        rest = (trace - high.astype(F32) - low.astype(F32)).astype(BF16)
+        both = dot16(jnp.concatenate([rest, low, high, *two(between)], axis=1), weave_ref[...])
+        for tile in range(count):
+            extended_ref[:, aligned(2 * k * size + tile * WIDE, WIDE)] = both[8 * tile : 8 * tile + 8]
+        hand_over(k).start()
 
     all_peers(notes_ref, note_recv).wait()
     entering = jnp.zeros((8, LANES), F32)
@@ -506,23 +540,42 @@
     def _(step):
         entry(step).start()
 
-    own_entry = pltpu.make_async_copy(entry_ref.at[part], carry_hbm.at[0], own_sem.at[1])
+    own_entry = pltpu.make_async_copy(entry_ref.at[part], carry_out.at[0], own_sem.at[1])
     own_entry.start()
     for k in range(2):
         ships[k].wait_send()
     for k in range(2, 6):
         ships[k].wait()
+    own = []
     for half, slots in ((0, (3, 4)), (1, (2, 5))):
-        own = partial_ref[half_at(part, half), :]
-        own_ref[half * half_leaves : (half + 1) * half_leaves, :] = own + pieces_ref[slots[0]] + pieces_ref[slots[1]]
-    own_store = pltpu.make_async_copy(own_ref, own_hbm, own_sem.at[0])
-    own_store.start()
-
-    @pl.loop(0, 2 * parts)
-    def _(step):
-        store(step, aligned(step * half_rows, half_rows)).wait()
-
-    own_store.wait()
+        own.append(partial_ref[half_at(part, half), :] + pieces_ref[slots[0]] + pieces_ref[slots[1]])
+    own = jnp.concatenate(own, axis=0)
+    own_rows = own.shape[0]
+    fraction = dot_exact(own, ones("weave"))
+    within = dot_exact(own, ones("lane"))
+    ends = jnp.broadcast_to(within[:, WIDE - 1 :], (own_rows, LANES))
+    high, low = two(ends)
+    rest = (ends - high.astype(F32) - low.astype(F32)).astype(BF16)
+    earlier = ones("row")[:, :LANES]
+    before = dot16(earlier, rest) + dot16(earlier, low) + dot16(earlier, high)
+    for half in range(2):
+        at = slice(half * LANES, (half + 1) * LANES)
+        out = pl.ds(half, own_rows, stride=2)
+        fraction_ref[out, :] = fraction[:, at]
+        running_ref[out, :] = (within[:, at] + before) * scale
+    own_stores = [
+        pltpu.make_async_copy(fraction_ref, fraction_out, own_sem.at[0]),
+        pltpu.make_async_copy(running_ref, running_out, own_sem.at[2]),
+    ]
+    for store in own_stores:
+        store.start()
+
+    @pl.loop(0, CHUNKS)
+    def _(k):
+        hand_over(k).wait()
+
+    for store in own_stores:
+        store.wait()
     own_entry.wait()
 
     @pl.loop(1, parts)
@@ -534,114 +587,62 @@
 
 
 def output_kernel(
-    scale, x_hbm, coset_hbm, own_hbm, carry_hbm, weave_hbm, order_hbm, lane_hbm, row_hbm, extended_hbm, fraction_hbm, running_hbm,
-    x_ref, coset_ref, own_ref, carry_ref, weave_ref, order_ref, lane_ref, row_ref, extended_ref, fraction_ref, running_ref,
-    load_sem, x_sem, coset_sem, out_sem, store_sem,
+    scale, extended_in, fraction_in, running_in, carry_ref, extended_hbm, fraction_hbm, running_ref, store_sem
 ):
-    rows = x_ref.shape[1]
-    chunks = x_sem.shape[0]
-    size = rows // chunks
-    small = (
-        (weave_hbm, weave_ref), (own_hbm, own_ref), (carry_hbm, carry_ref), (order_hbm, order_ref),
-        (lane_hbm, lane_ref), (row_hbm, row_ref),
-    )
-    loads = [pltpu.make_async_copy(*pair, load_sem.at[k]) for k, pair in enumerate(small)]
-
-    def rows_in(k):
-        at = aligned(k * size, size)
-        return (
-            pltpu.make_async_copy(x_hbm.at[:, at], x_ref.at[:, at], x_sem.at[k]),
-            pltpu.make_async_copy(coset_hbm.at[:, at], coset_ref.at[:, at], coset_sem.at[k]),
-        )
-
-    def rows_out(k):
-        at = aligned(2 * k * size, 2 * size)
-        return pltpu.make_async_copy(extended_ref.at[:, at], extended_hbm.at[:, at], out_sem.at[k])
-
-    loads[0].start()
-    for k in range(chunks):
-        for load in rows_in(k):
-            load.start()
-    for load in loads[1:]:
-        load.start()
-    loads[0].wait()
-
-    @pl.loop(0, chunks)
-    def _(k):
-        for load in rows_in(k):
-            load.wait()
-        count = size // LANES
-        slices = [aligned(k * size + tile * LANES, LANES) for tile in range(count)]
-        own = jnp.concatenate([x_ref[:, at] for at in slices], axis=0)
-        between = jnp.concatenate([coset_ref[:, at] for at in slices], axis=0)
-        high, low = two(own)
-        rest = (own - high.astype(F32) - low.astype(F32)).astype(BF16)
-        both = dot16(jnp.concatenate([rest, low, high, *two(between)], axis=1), weave_ref[...])
-        for tile in range(count):
-            extended_ref[:, aligned(2 * k * size + tile * WIDE, WIDE)] = both[8 * tile : 8 * tile + 8]
-        rows_out(k).start()
-
-    for load in loads[1:]:
-        load.wait()
-    own = own_ref[...]
-    size_own = own.shape[0]
-    fraction = dot_exact(own, order_ref[...])
-    within = dot_exact(own, lane_ref[...])
-    ends = jnp.broadcast_to(within[:, WIDE - 1 :], (size_own, LANES))
-    high, low = two(ends)
-    rest = (ends - high.astype(F32) - low.astype(F32)).astype(BF16)
-    before = dot16(row_ref[...], rest) + dot16(row_ref[...], low) + dot16(row_ref[...], high)
-    before = before + jnp.sum(carry_ref[...])
-    for half in range(2):
-        at = slice(half * LANES, (half + 1) * LANES)
-        out = pl.ds(half, size_own, stride=2)
-        fraction_ref[out, :] = fraction[:, at]
-        running_ref[out, :] = (within[:, at] + before) * scale
-    stores = [
-        pltpu.make_async_copy(fraction_ref, fraction_hbm, store_sem.at[0]),
-        pltpu.make_async_copy(running_ref, running_hbm, store_sem.at[1]),
-    ]
-    for store in stores:
-        store.start()
-
-    @pl.loop(0, chunks)
-    def _(k):
-        rows_out(k).wait()
-
-    for store in stores:
-        store.wait()
+    size = extended_in.shape[1] // CHUNKS
+
+    def store(k):
+        at = pl.ds(k * size, size)
+        return pltpu.make_async_copy(extended_in.at[:, at], extended_hbm.at[:, at], store_sem.at[k])
+
+    for k in range(CHUNKS):
+        store(k).start()
+    store_fraction = pltpu.make_async_copy(fraction_in, fraction_hbm, store_sem.at[CHUNKS])
+    store_fraction.start()
+    running_ref[...] = running_in[...] + jnp.sum(carry_ref[...]) * scale
+    for k in range(CHUNKS):
+        store(k).wait()
+    store_fraction.wait()
 
 
 def local(groups, parts, trace_values, challenges, multiplicity, table_index):
     columns, rows = trace_values.shape
     total = groups * rows
     (high, low), places = matrices(total, groups)
+    scale = 1.0 / (2 * total)
     leaves = rows // LEAF
     parents = leaves // RADIX
-    smem = pl.BlockSpec(memory_space=pltpu.SMEM)
+    vmem = pl.BlockSpec(memory_space=pltpu.VMEM)
     hbm = pl.BlockSpec(memory_space=pl.ANY)
     dma = pltpu.SemaphoreType.DMA
     size = leaves // parts
     tile = lambda *lead: pltpu.VMEM(lead + (columns, LANES), F32)
-    coset, own, carry = pl.pallas_call(
-        functools.partial(main_kernel, groups, parts, places, BATCH),
+    sources = (challenges, trace_values, multiplicity, table_index, jnp.asarray(high), jnp.asarray(low))
+    sources = [pltpu.with_memory_space_constraint(source, pltpu.HBM) for source in sources]
+    extended, fraction, running, carry = pl.pallas_call(
+        functools.partial(main_kernel, groups, parts, scale, places),
         out_shape=(
-            jax.ShapeDtypeStruct((columns, rows), F32),
-            jax.ShapeDtypeStruct((size, WIDE), F32),
-            jax.ShapeDtypeStruct((parts, columns, LANES), F32),
+            pltpu.VMEM((columns, 2 * rows), F32),
+            pltpu.VMEM((2 * size, LANES), F32),
+            pltpu.VMEM((2 * size, LANES), F32),
+            pltpu.VMEM((parts, columns, LANES), F32),
         ),
-        in_specs=[smem] + [hbm] * 5,
-        out_specs=(hbm, hbm, hbm),
+        in_specs=[hbm] * 6,
+        out_specs=(hbm, hbm, hbm, hbm),
         scratch_shapes=[
+            pltpu.SMEM((columns,), F32),
             pltpu.VMEM((columns, rows + 2 * LEAF), F32),
             pltpu.VMEM((columns, 2 * rows), jnp.int32),
             pltpu.VMEM((columns, 2 * rows), jnp.int32),
             pltpu.VMEM(high.shape, BF16),
-            pltpu.VMEM(high.shape, BF16),
+            pltpu.VMEM(low.shape, BF16),
             pltpu.VMEM((columns, rows), F32),
+            pltpu.VMEM((columns, 2 * rows), F32),
+            pltpu.VMEM((5 * LEAF, WIDE), BF16),
             pltpu.VMEM((columns * parents, WIDE), F32),
             pltpu.VMEM((columns * parents, WIDE), F32),
-            pltpu.VMEM((size, WIDE), F32),
+            pltpu.VMEM((2 * size, LANES), F32),
+            pltpu.VMEM((2 * size, LANES), F32),
             pltpu.VMEM((leaves, WIDE), F32),
             pltpu.VMEM((leaves, WIDE), F32),
             tile(groups),
@@ -651,42 +652,25 @@
             tile(2 * parts),
             tile(groups),
             tile(parts),
-            dma, dma((4,)), dma((2, parts)), dma((2 * parts,)), dma((2,)),
+            dma((parts,)), dma((5,)), dma((2, parts)), dma((CHUNKS,)), dma((3,)),
             dma, dma, dma((2,)), dma((2,)),
             dma((6,)), dma((6,)), dma, dma, dma((parts,)), dma((parts,)),
         ],
         compiler_params=pltpu.CompilerParams(
-            collective_id=0, has_side_effects=True, vmem_limit_bytes=56 * 2**20
+            collective_id=0, has_side_effects=True, vmem_limit_bytes=48 * 2**20
         ),
         name="main",
-    )(challenges, trace_values, multiplicity, table_index, high, low)
-    order = high[slice(*places["weave"])]
-    weave_rows = order.reshape(2, LEAF, WIDE)[np.array((0, 0, 0, 1, 1))].reshape(-1, WIDE)
-    lane_sum = (order.astype(np.float32) @ np.triu(np.ones((WIDE, WIDE), np.float32))).astype(ml_dtypes.bfloat16)
-    row_sum = np.tril(np.ones((size, size)), -1).astype(ml_dtypes.bfloat16)
+    )(*sources)
     flat = jax.ShapeDtypeStruct((2 * size, LANES), F32)
     extended, fraction, running = pl.pallas_call(
-        functools.partial(output_kernel, 1.0 / (2 * total)),
+        functools.partial(output_kernel, scale),
         out_shape=(jax.ShapeDtypeStruct((columns, 2 * rows), F32), flat, flat),
-        in_specs=[hbm] * 8,
-        out_specs=(hbm, hbm, hbm),
-        scratch_shapes=[
-            pltpu.VMEM((columns, rows), F32),
-            pltpu.VMEM((columns, rows), F32),
-            pltpu.VMEM((size, WIDE), F32),
-            tile(parts),
-            pltpu.VMEM((5 * LEAF, WIDE), BF16),
-            pltpu.VMEM((WIDE, WIDE), BF16),
-            pltpu.VMEM((WIDE, WIDE), BF16),
-            pltpu.VMEM((size, size), BF16),
-            pltpu.VMEM((columns, 2 * rows), F32),
-            pltpu.VMEM((2 * size, LANES), F32),
-            pltpu.VMEM((2 * size, LANES), F32),
-            dma((6,)), dma((CHUNKS,)), dma((CHUNKS,)), dma((CHUNKS,)), dma((2,)),
-        ],
-        compiler_params=pltpu.CompilerParams(vmem_limit_bytes=60 * 2**20),
-        name="weave",
-    )(trace_values, coset, own, carry, weave_rows, order, lane_sum, row_sum)
+        in_specs=[hbm, hbm, vmem, vmem],
+        out_specs=(hbm, hbm, vmem),
+        scratch_shapes=[dma((CHUNKS + 1,))],
+        compiler_params=pltpu.CompilerParams(vmem_limit_bytes=16 * 2**20),
+        name="finish",
+    )(extended, fraction, running, carry)
     return extended, fraction.reshape(-1), running.reshape(-1)
 
 

time: 35.5 us -> 31.8 us (0.90)
  Pallas kernels: 34.7 us -> 31 us
    pallas_call x2, Pallas kernels: 34.7 us -> 31 us  [the longest x1 28.3 us: local(): pl.pallas_call(functools.partial(main_kernel, groups, parts, scale, place...]
where the time goes in v4:
time: 31.8 us; the launch traced here: 31.6 us
  Pallas kernels  31 us (97%)
  between operations  0.64 us (2%)
    pallas_call x1, Pallas kernels, local(): pl.pallas_call(functools.partial(main_kernel, groups, parts, scale, place...  28.3 us
    pallas_call x1, Pallas kernels, local(): pl.pallas_call(functools.partial(output_kernel, scale), out_shape=(jax.Sh...  2.74 us

profile of v4, /device:TPU:0, one launch (start us, length us, event | category | flops | bytes accessed | tf_op | source)
XLA Modules:
  0.0 31.6 jit_solution(4440656491552454752)
XLA Ops:
  0.6 28.3 %main.1 = (f32[8,131072]{1,0:T(8,128)S(1)}, f32[256,128]{1,0:T(8,128)S(1)}, f32[256,128]{1,0:T(8,128)S(1)}, f32[4,8,128]{2,1,0:T(8,128)S(1)}) custom-call(f32[8]{0:T(128)} %challenge_hbm.1, f32[8,65536]{1,0:T(8,128)} %x_hbm.1, s32[8,131072]{1,0:T(8,128)} %multiplicity_hbm.1, s32[8,131072]{1,0:T(8,128)} %index_hbm.1, ...), custom_call_target="tpu_custom_call" | custom-call | tf_op jit(solution)/shard_map/main/pallas_call | solution.py:622
  28.9 2.7 %finish.1 = (f32[8,131072]{1,0:T(8,128)}, f32[256,128]{1,0:T(8,128)}, f32[256,128]{1,0:T(8,128)}) custom-call(f32[8,131072]{1,0:T(8,128)S(1)} %get-tuple-element.10.extended_in, f32[256,128]{1,0:T(8,128)S(1)} %get-tuple-element.11.fraction_in, f32[256,128]{1,0:T(8,128)S(1)} %get-tuple-element.12.running_in, f32[4,8,128]{2,1,0:T(8,128)S(1)} %get-tuple-element.13.carry_ref), custom_call_target="tpu_custom_call" | custom-call | tf_op jit(solution)/shard_map/finish/pallas_call | solution.py:665

commit v5 on v4

--- a/solution.py
+++ b/solution.py
@@ -19,10 +19,8 @@
 TABLE_BATCH = 2
 TABLE_AFTER = 2
 CHUNKS = 4
-FAR_FIRST = 2 + 1 * 4 + 3 * 16 + 0 * 64
-STEPS = ((2, 0), (2, 1), (1, 1), (3, 0), (1, 0), (3, 1), (0, 0), (0, 1))
-QUARTERS = sum(quarter * 4**step for step, (quarter, _) in enumerate(STEPS))
-HALVES = sum(half * 2**step for step, (_, half) in enumerate(STEPS))
+
+QUARTERS = 2 + 1 * 4 + 3 * 16 + 0 * 64
 MESH = pl.DeviceIdType.MESH
 F32 = jnp.float32
 BF16 = jnp.bfloat16
@@ -88,10 +86,9 @@
     c2p = child_to_parent()
     three = np.arange(3 * RADIX) - RADIX
     one = np.arange(RADIX)
-    top_far = np.zeros((blocks * NODES, WIDE))
-    top_far[:, : per_device * NODES] = far_weights(
-        np.arange(blocks), np.arange(per_device), top, total, blocks
-    )
+    here = per_device * NODES
+    top_far = far_weights(np.arange(blocks), np.arange(per_device), top, total, blocks)
+    top_far = top_far.reshape(-1, LANES, here).transpose(1, 0, 2).reshape(LANES, -1)
     top_down = np.zeros((per_device, LANES, WIDE))
     for block in range(per_device):
         top_down[block, block * NODES : (block + 1) * NODES] = c2p.T
@@ -196,8 +193,9 @@
 
 
 def row_peer(me, step):
-    across = lax.rem(me // 8 + lax.rem(lax.shift_right_logical(FAR_FIRST, 2 * (step // 8)), 4), 4)
-    along = lax.rem(me // 2 + lax.rem(lax.shift_right_logical(FAR_FIRST, 2 * lax.rem(step // 2, 4)), 4), 4)
+    far_first = (2, 1, 3, 0)
+    across = lax.rem(me // 8 + far_first[step // 8], 4)
+    along = lax.rem(me // 2 + far_first[step // 2 % 4], 4)
     core = lax.rem(me + 1 + step, 2)
     return 8 * across + 2 * along + core
 
@@ -207,8 +205,7 @@
     for axis, size in axes:
         me = lax.axis_index(axis)
 
-        @pl.loop(1, size)
-        def _(step):
+        for step in range(1, size):
             peer = lax.rem(me + step, size)
             pl.semaphore_signal(barrier, inc=1, device_id={axis: peer}, device_id_type=MESH)
 
@@ -336,8 +333,7 @@
     edge(0).start()
     edge(1).start()
 
-    @pl.loop(0, groups - 1)
-    def _(step):
+    for step in range(groups - 1):
         message(step).start()
 
     load_challenges.wait()
@@ -398,10 +394,15 @@
             there = gathered_ref[lax.rem(me + per_tile * k + place, groups)]
             tile = jnp.where(group // tops == place, there, tile)
         pieces.append(tile)
-    top_local = dot_pieces(
-        two(jnp.concatenate(pieces, axis=1)), [piece[:, :LANES] for piece in weights("top")]
-    )
-    top_pair = two(top_local)
+    top_local = dot_pieces(two(jnp.concatenate(pieces, axis=0)), weights("top"))
+    tile_of = lax.broadcasted_iota(jnp.int32, (8, WIDE), 1) // (tops * NODES)
+    picked = top_local[0:8]
+    for k in range(1, len(pieces)):
+        picked = jnp.where(tile_of == k, top_local[8 * k : 8 * k + 8], picked)
+    picked = picked[:, :LANES] + picked[:, LANES:]
+    for shift in (LANES // 2, LANES // 4):
+        picked = picked + pltpu.roll(picked, shift, 1)
+    top_pair = two(picked)
     expanded = []
     for g in range(tops):
         here = dot_pieces(top_pair, weights("top_down", LANES * g, LANES * g + LANES))
@@ -433,53 +434,51 @@
         ship(5, half_at(before_me, 1), before_me),
     )
 
-    def half_of(step):
-        quarter = lax.rem(part + lax.rem(lax.shift_right_logical(QUARTERS, 2 * step), 4), parts)
-        return 2 * quarter + lax.rem(lax.shift_right_logical(HALVES, step), 2)
-
-    def product(half):
-        start = half * half_rows
-        tiles = [x_ref[:, aligned(start + LEAF * j, LEAF)] for j in range(half_leaves + 2)]
-        sources = [jnp.concatenate(tiles[k : k + half_leaves : 2], axis=0) for k in range(4)]
+    part_leaves = leaves // parts
+
+    def quarter_of(step):
+        return lax.rem(part + lax.rem(lax.shift_right_logical(QUARTERS, 2 * step), 4), parts)
+
+    def product(quarter):
+        start = quarter * quarter_rows
+        tiles = [x_ref[:, aligned(start + LEAF * j, LEAF)] for j in range(part_leaves + 2)]
+        sources = [jnp.concatenate(tiles[k : k + part_leaves : 2], axis=0) for k in range(4)]
         expanded = []
-        for p in range(half_leaves // RADIX):
-            expanded += spread(local_ref[aligned(8 * (half * (half_leaves // RADIX) + p), 8), :], 2 * NODES)
+        for p in range(part_leaves // RADIX):
+            expanded += spread(local_ref[aligned(8 * (quarter * (part_leaves // RADIX) + p), 8), :], 2 * NODES)
         sources.append(jnp.concatenate(expanded, axis=0))
         pairs = [two(source) for source in sources]
         left = [jnp.concatenate([pair[k] for pair in pairs], axis=1) for k in range(2)]
         result = dot_pieces(left, weights("out"))
-        for j in range(half_leaves // 2):
+        for j in range(part_leaves // 2):
             coset_ref[:, aligned(start + 2 * LEAF * j, 2 * LEAF)] = result[8 * j : 8 * j + 8]
 
-    def sums(half):
+    def sums(quarter):
         total = jnp.zeros((8, LANES), F32)
-        for j in range(half_leaves // 8):
+        for j in range(part_leaves // 8):
             terms = []
             for k in range(8):
-                value = coset_ref[:, aligned(half * half_rows + LEAF * (8 * j + k), LEAF)]
+                value = coset_ref[:, aligned(quarter * quarter_rows + LEAF * (8 * j + k), LEAF)]
                 terms.append(invert(weight + value * value))
-            at = aligned(half * half_leaves + 8 * j, 8)
+            at = aligned(quarter * part_leaves + 8 * j, 8)
             odd = column_sums(terms) - table_ref[at, LANES:]
             partial_ref[at, LANES:] = odd
             total = total + (odd + partial_ref[at, 0:LANES])
-        note_ref[half] = total
-
-    product(half_of(0))
-
-    @pl.loop(1, 2 * parts)
+        note_ref[quarter] = total
+
+    @pl.loop(0, parts)
     def _(step):
-        half = half_of(step - 1)
-        sums(half)
-        product(half_of(step))
-        for k in range(4):
-
-            @pl.when(step == k + 1)
-            def _(k=k):
-                ships[k].start()
-
-    sums(half_of(2 * parts - 1))
-
-    totals = [note_ref[2 * p] + note_ref[2 * p + 1] for p in range(parts)]
+        quarter = quarter_of(step)
+        product(quarter)
+        sums(quarter)
+        for k, ready in enumerate(((0, 1), (2,), (3,))):
+
+            @pl.when(step == k)
+            def _(ready=ready):
+                for one in ready:
+                    ships[one].start()
+
+    totals = [note_ref[p] for p in range(parts)]
     notes_ref[me] = (totals[0] + totals[1]) + (totals[2] + totals[3])
 
     def note(step):
@@ -495,8 +494,7 @@
             recv_sem=entry_recv.at[step], device_id={"cols": peer}, device_id_type=MESH,
         )
 
-    @pl.loop(0, groups - 1)
-    def _(step):
+    for step in range(groups - 1):
         note(step).start()
 
     for k in (4, 5):
@@ -536,8 +534,7 @@
         entry_ref[p] = entering
         entering = entering + totals[p]
 
-    @pl.loop(1, parts)
-    def _(step):
+    for step in (2, 1, 3):
         entry(step).start()
 
     own_entry = pltpu.make_async_copy(entry_ref.at[part], carry_out.at[0], own_sem.at[1])
@@ -578,8 +575,7 @@
         store.wait()
     own_entry.wait()
 
-    @pl.loop(1, parts)
-    def _(step):
+    for step in range(1, parts):
         entry(step).wait()
 
     all_peers(gathered_ref, send_sem).wait()

time: 31.8 us -> 30.3 us (0.953)
  Pallas kernels: 31 us -> 29.5 us
    pallas_call x1, Pallas kernels: 28.3 us -> 26.8 us  [local(): pl.pallas_call(functools.partial(main_kernel, groups, parts, scale, place...]
where the time goes in v5:
time: 30.3 us; the launch traced here: 30.2 us
  Pallas kernels  29.5 us (97%)
  between operations  0.64 us (2%)
    pallas_call x1, Pallas kernels, local(): pl.pallas_call(functools.partial(main_kernel, groups, parts, scale, place...  26.8 us
    pallas_call x1, Pallas kernels, local(): pl.pallas_call(functools.partial(output_kernel, scale), out_shape=(jax.Sh...  2.74 us

profile of v5, /device:TPU:0, one launch (start us, length us, event | category | flops | bytes accessed | tf_op | source)
XLA Modules:
  0.0 30.2 jit_solution(6568936819279052419)
XLA Ops:
  0.6 26.8 %main.1 = (f32[8,131072]{1,0:T(8,128)S(1)}, f32[256,128]{1,0:T(8,128)S(1)}, f32[256,128]{1,0:T(8,128)S(1)}, f32[4,8,128]{2,1,0:T(8,128)S(1)}) custom-call(f32[8]{0:T(128)} %challenge_hbm.1, f32[8,65536]{1,0:T(8,128)} %x_hbm.1, s32[8,131072]{1,0:T(8,128)} %multiplicity_hbm.1, s32[8,131072]{1,0:T(8,128)} %index_hbm.1, ...), custom_call_target="tpu_custom_call" | custom-call | tf_op jit(solution)/shard_map/main/pallas_call | solution.py:618
  27.4 2.7 %finish.1 = (f32[8,131072]{1,0:T(8,128)}, f32[256,128]{1,0:T(8,128)}, f32[256,128]{1,0:T(8,128)}) custom-call(f32[8,131072]{1,0:T(8,128)S(1)} %get-tuple-element.10.extended_in, f32[256,128]{1,0:T(8,128)S(1)} %get-tuple-element.11.fraction_in, f32[256,128]{1,0:T(8,128)S(1)} %get-tuple-element.12.running_in, f32[4,8,128]{2,1,0:T(8,128)S(1)} %get-tuple-element.13.carry_ref), custom_call_target="tpu_custom_call" | custom-call | tf_op jit(solution)/shard_map/finish/pallas_call | solution.py:661

commit v6 on v5

--- a/solution.py
+++ b/solution.py
@@ -483,8 +483,8 @@
 
     def note(step):
         return pltpu.make_async_remote_copy(
-            src_ref=notes_ref.at[me], dst_ref=notes_ref.at[me], send_sem=note_send, recv_sem=note_recv,
-            device_id={"rows": row_peer(me, step)}, device_id_type=MESH,
+            src_ref=notes_ref.at[me], dst_ref=notes_ref.at[me], send_sem=note_send.at[step],
+            recv_sem=note_recv.at[me], device_id={"rows": row_peer(me, step)}, device_id_type=MESH,
         )
 
     def entry(step):
@@ -495,7 +495,10 @@
         )
 
     for step in range(groups - 1):
-        note(step).start()
+
+        @pl.when(row_peer(me, step) > me)
+        def _(step=step):
+            note(step).start()
 
     for k in (4, 5):
         ships[k - 4].wait_recv()
@@ -526,7 +529,10 @@
             extended_ref[:, aligned(2 * k * size + tile * WIDE, WIDE)] = both[8 * tile : 8 * tile + 8]
         hand_over(k).start()
 
-    all_peers(notes_ref, note_recv).wait()
+    @pl.loop(0, me)
+    def _(k):
+        pltpu.make_async_copy(notes_ref.at[k], notes_ref.at[k], note_recv.at[k]).wait()
+
     entering = jnp.zeros((8, LANES), F32)
     for k in range(groups):
         entering = entering + jnp.where(k < me, notes_ref[k], 0.0)
@@ -579,7 +585,11 @@
         entry(step).wait()
 
     all_peers(gathered_ref, send_sem).wait()
-    all_peers(notes_ref, note_send).wait()
+    for step in range(groups - 1):
+
+        @pl.when(row_peer(me, step) > me)
+        def _(step=step):
+            note(step).wait_send()
 
 
 def output_kernel(
@@ -650,7 +660,7 @@
             tile(parts),
             dma((parts,)), dma((5,)), dma((2, parts)), dma((CHUNKS,)), dma((3,)),
             dma, dma, dma((2,)), dma((2,)),
-            dma((6,)), dma((6,)), dma, dma, dma((parts,)), dma((parts,)),
+            dma((6,)), dma((6,)), dma((groups,)), dma((groups,)), dma((parts,)), dma((parts,)),
         ],
         compiler_params=pltpu.CompilerParams(
             collective_id=0, has_side_effects=True, vmem_limit_bytes=48 * 2**20

time: 30.3 us -> 29.7 us (0.980)
  Pallas kernels: 29.5 us -> 28.9 us
    pallas_call x1, Pallas kernels: 26.8 us -> 26.2 us  [local(): pl.pallas_call(functools.partial(main_kernel, groups, parts, scale, place...]
where the time goes in v6:
time: 29.7 us; the launch traced here: 29.5 us
  Pallas kernels  28.9 us (97%)
  between operations  0.64 us (2%)
    pallas_call x1, Pallas kernels, local(): pl.pallas_call(functools.partial(main_kernel, groups, parts, scale, place...  26.2 us
    pallas_call x1, Pallas kernels, local(): pl.pallas_call(functools.partial(output_kernel, scale), out_shape=(jax.Sh...  2.74 us

profile of v6, /device:TPU:0, one launch (start us, length us, event | category | flops | bytes accessed | tf_op | source)
XLA Modules:
  0.0 29.5 jit_solution(1614356910272077693)
XLA Ops:
  0.6 26.2 %main.1 = (f32[8,131072]{1,0:T(8,128)S(1)}, f32[256,128]{1,0:T(8,128)S(1)}, f32[256,128]{1,0:T(8,128)S(1)}, f32[4,8,128]{2,1,0:T(8,128)S(1)}) custom-call(f32[8]{0:T(128)} %challenge_hbm.1, f32[8,65536]{1,0:T(8,128)} %x_hbm.1, s32[8,131072]{1,0:T(8,128)} %multiplicity_hbm.1, s32[8,131072]{1,0:T(8,128)} %index_hbm.1, ...), custom_call_target="tpu_custom_call" | custom-call | tf_op jit(solution)/shard_map/main/pallas_call | solution.py:628
  26.8 2.7 %finish.1 = (f32[8,131072]{1,0:T(8,128)}, f32[256,128]{1,0:T(8,128)}, f32[256,128]{1,0:T(8,128)}) custom-call(f32[8,131072]{1,0:T(8,128)S(1)} %get-tuple-element.10.extended_in, f32[256,128]{1,0:T(8,128)S(1)} %get-tuple-element.11.fraction_in, f32[256,128]{1,0:T(8,128)S(1)} %get-tuple-element.12.running_in, f32[4,8,128]{2,1,0:T(8,128)S(1)} %get-tuple-element.13.carry_ref), custom_call_target="tpu_custom_call" | custom-call | tf_op jit(solution)/shard_map/finish/pallas_call | solution.py:671

commit v7 on v6

--- a/solution.py
+++ b/solution.py
@@ -515,8 +515,7 @@
         at = aligned(2 * k * size, 2 * size)
         return pltpu.make_async_copy(extended_ref.at[:, at], extended_out.at[:, at], store_sem.at[k])
 
-    @pl.loop(0, CHUNKS)
-    def _(k):
+    def interleave(k):
         count = size // LANES
         trace = [x_ref[:, aligned(LEAF + k * size + tile * LANES, LANES)] for tile in range(count)]
         trace = jnp.concatenate(trace, axis=0)
@@ -529,6 +528,8 @@
             extended_ref[:, aligned(2 * k * size + tile * WIDE, WIDE)] = both[8 * tile : 8 * tile + 8]
         hand_over(k).start()
 
+    pl.loop(0, CHUNKS // 2)(interleave)
+
     @pl.loop(0, me)
     def _(k):
         pltpu.make_async_copy(notes_ref.at[k], notes_ref.at[k], note_recv.at[k]).wait()
@@ -545,6 +546,7 @@
 
     own_entry = pltpu.make_async_copy(entry_ref.at[part], carry_out.at[0], own_sem.at[1])
     own_entry.start()
+    pl.loop(CHUNKS // 2, CHUNKS)(interleave)
     for k in range(2):
         ships[k].wait_send()
     for k in range(2, 6):

time: 29.7 us -> 29.5 us (level)
  the two profiles are of different devices: /device:TPU:0 before, /device:TPU:2 now
where the time goes in v7:
time: 29.5 us; the launch traced here: 29.3 us
  Pallas kernels  28.7 us (97%)
  between operations  0.64 us (2%)
    pallas_call x1, Pallas kernels, local(): pl.pallas_call(functools.partial(main_kernel, groups, parts, scale, place...  26 us
    pallas_call x1, Pallas kernels, local(): pl.pallas_call(functools.partial(output_kernel, scale), out_shape=(jax.Sh...  2.74 us

profile of v7, /device:TPU:2, one launch (start us, length us, event | category | flops | bytes accessed | tf_op | source)
XLA Modules:
  0.0 29.3 jit_solution(7963345329725432274)
XLA Ops:
  0.6 26.0 %main.1 = (f32[8,131072]{1,0:T(8,128)S(1)}, f32[256,128]{1,0:T(8,128)S(1)}, f32[256,128]{1,0:T(8,128)S(1)}, f32[4,8,128]{2,1,0:T(8,128)S(1)}) custom-call(f32[8]{0:T(128)} %challenge_hbm.1, f32[8,65536]{1,0:T(8,128)} %x_hbm.1, s32[8,131072]{1,0:T(8,128)} %multiplicity_hbm.1, s32[8,131072]{1,0:T(8,128)} %index_hbm.1, ...), custom_call_target="tpu_custom_call" | custom-call | tf_op jit(solution)/shard_map/main/pallas_call | solution.py:630
  26.6 2.7 %finish.1 = (f32[8,131072]{1,0:T(8,128)}, f32[256,128]{1,0:T(8,128)}, f32[256,128]{1,0:T(8,128)}) custom-call(f32[8,131072]{1,0:T(8,128)S(1)} %get-tuple-element.10.extended_in, f32[256,128]{1,0:T(8,128)S(1)} %get-tuple-element.11.fraction_in, f32[256,128]{1,0:T(8,128)S(1)} %get-tuple-element.12.running_in, f32[4,8,128]{2,1,0:T(8,128)S(1)} %get-tuple-element.13.carry_ref), custom_call_target="tpu_custom_call" | custom-call | tf_op jit(solution)/shard_map/finish/pallas_call | solution.py:673
